TPU v7x, 128 devices: a whole 4x4x4 slice. The times are simulated.
128 devices in a mesh: gx: 32 (over x_lo, z, y), gy: 4 (over x_hi, core).
Axes of the slice: x: 4 (x_hi: 2, x_lo: 2; x = x_hi * 2 + x_lo), y: 4, z: 4, core: 2. Of those that a mesh axis runs over, the one named last changes fastest.
Arguments:
- field_in: bfloat16 [3, 128, 32, 128], P(None, 'gx', 'gy'), may hold values from -6 to 6
- cotangent: bfloat16 [3, 128, 32, 128], P(None, 'gx', 'gy'), may hold values from -6 to 6
- kernel_one: bfloat16 [64, 3, 3, 3, 3], replicated, may hold values from -0.625 to 0.625
- kernel_two: bfloat16 [27, 4096], replicated, may hold values from -0.15625 to 0.15625
- kernel_three: bfloat16 [27, 4096], replicated, may hold values from -0.15625 to 0.15625
- kernel_four: bfloat16 [3, 64, 3, 3, 3], replicated, may hold values from -0.15625 to 0.15625
Outputs:
- output: float32 [3, 128, 32, 128], P(None, 'gx', 'gy')
- grad_one: float32 [64, 3, 3, 3, 3], replicated
- grad_two: float32 [27, 4096], replicated
- grad_three: float32 [27, 4096], replicated
- grad_four: float32 [3, 64, 3, 3, 3], replicated
All inputs are finite; a program needn't handle non-finite values.
Results may differ from a plain program's by a relative error of at most 0.015.
Values may be sent and summed in bfloat16 or wider, within the bound.
No kernel may reach another device: no remote copies, remote signals or barrier semaphores. Data moves between devices by JAX's collectives and lax.ppermute only.
A program may use at most 128 MiB of HBM per device.

v0:
```python
import math

import jax
import jax.numpy as jnp
from jax import lax
from jax.experimental import pallas as pl
from jax.experimental.pallas import tpu as pltpu
from jax.sharding import PartitionSpec as P

F32 = jnp.float32
BF16 = jnp.bfloat16
AXES = ("gx", "gy")
HALO = 8
CH = 64
LANES = 128
FIELD_ROWS = (0, 2, 1, None)
GRADIENT_ROWS = (0, 2, None, 1)


def shifted(block, axis, steps):
    count = lax.axis_size(axis)
    return lax.ppermute(block, axis, [(i, (i + steps) % count) for i in range(count)])


def toeplitz_rows(taps):
    low = jnp.pad(taps, ((0, 0), (0, 1), (0, 0), (0, 0), (0, 0)))
    high = jnp.pad(taps, ((0, 0), (1, 0), (0, 0), (0, 0), (0, 0)))
    both = jnp.stack([low, high])
    both = jnp.transpose(both, (0, 3, 4, 1, 2, 5))
    return both.reshape(6 * taps.shape[3], 12 * taps.shape[4])


def weights_kernel(two_ref, three_ref, t2_ref, t2b_ref, t3_ref, t3b_ref):
    row, column = (lax.broadcasted_iota(jnp.int32, (CH, CH), axis) for axis in range(2))
    eye = (row == column).astype(BF16)
    zero = jnp.zeros((CH, CH), BF16)
    for source, forward, backward in (
        (two_ref, t2_ref, t2b_ref),
        (three_ref, t3_ref, t3b_ref),
    ):
        for a in range(3):
            for e in range(3):
                taps = [source[9 * a + 3 * b + e] for b in range(3)]
                plain = jnp.concatenate([tap.astype(F32) for tap in taps + [zero]], axis=1)
                turn = contract(eye, jnp.concatenate(taps[::-1] + [zero], axis=0))
                for target, values, at, lane in (
                    (forward, plain, CH * e, 4 * CH * a),
                    (backward, turn, CH * (2 - e), 4 * CH * (2 - a)),
                ):
                    lanes = slice(lane, lane + 4 * CH)
                    target[at : at + CH, lanes] = values.astype(BF16)
                    moved = pltpu.roll(values, CH, 1).astype(BF16)
                    target[at + 3 * CH : at + 4 * CH, lanes] = moved


def toeplitz_window(taps, places):
    taps = jnp.pad(taps, ((0, 0),) * 4 + ((0, 1),))
    zero = jnp.zeros_like(taps[:, :, :, 0])
    taps = jnp.concatenate([zero if e is None else taps[:, :, :, e] for e in places], axis=3)
    rows = [
        jnp.pad(taps, ((0, 0), (dx, 1 - dx), (dy, 1 - dy), (0, 0)))
        for dx in range(2)
        for dy in range(2)
    ]
    return jnp.stack(rows).reshape(4 * taps.shape[0], 256)


def swapped(taps):
    return jnp.swapaxes(jnp.flip(taps, (0, 1, 2)), 3, 4)


def leaky(values):
    return values * (0.55 + 0.45 * jnp.tanh(0.5 * values))


def slope(values):
    sigma = 0.5 + 0.5 * jnp.tanh(0.5 * values)
    return 0.1 + 0.9 * sigma * (1.0 + values * (1.0 - sigma))


def turned(values, steps):
    return pltpu.roll(values, steps % LANES, values.ndim - 1)


def window_of(source, x, y):
    rows = [source[x + r, pl.ds(y, 4)].reshape(4 * CH, LANES) for r in range(4)]
    return jnp.concatenate(
        [jnp.concatenate([rows[a], rows[a + 1]], axis=1) for a in range(3)], axis=0
    )


def product_pair(source, weights, x, y):
    window = jnp.concatenate([window_of(source, x, y), window_of(source, x, y + 2)], axis=1)
    return jnp.dot(weights[...], window, preferred_element_type=F32)


def column_of(product, dx, dy, step):
    out = product.shape[0] // 6
    rows, lane = 3 * out * (dy % 2), LANES * (dx + 2 * (dy // 2))
    first, second, third = (
        product[rows + out * e : rows + out * (e + 1), lane : lane + LANES] for e in range(3)
    )
    return turned(first, step) + second + turned(third, -step)


def pipelined(count, most, product, finish, even, odd):
    odd[...] = jnp.zeros(odd.shape, odd.dtype)
    pairs = count // 2
    many = next(m for m in range(most, 0, -1) if pairs % m == 0)

    @pl.loop(0, pairs // many)
    def _(v):
        for w in range(many):
            t = 2 * (v * many + w)
            even[...] = product(t)
            finish(jnp.maximum(t - 1, 0) if w == 0 else t - 1, odd)
            odd[...] = product(t + 1)
            finish(t, even)

    if count % 2:
        even[...] = product(count - 1)
        finish(count - 2, odd)
        finish(count - 1, even)
    else:
        finish(count - 1, odd)


def window_row(source, weights, x, y, blocks):
    parts = []
    for k in range(blocks):
        rows = [source[x + r, pl.ds(y + 2 * k, 4)].reshape(64, LANES) for r in range(4)]
        parts.append(jnp.concatenate(rows, axis=0))
    return jnp.dot(weights[...], jnp.concatenate(parts, axis=1), preferred_element_type=F32)


def window_column(product, dx, y):
    at, lane = CH * (2 * dx + y % 2), LANES * (y // 2)
    return product[at : at + CH, lane : lane + LANES]


def line(source, x, y, count):
    return jnp.concatenate([source[x, y + k] for k in range(count)], axis=1)


def neighbour_lines(source, x, y, count):
    return [line(source, x + a - 1, y + b - 1, count) for a in range(3) for b in range(3)]


def contract(left, right):
    return lax.dot_general(left, right, (((1,), (1,)), ((), ())), preferred_element_type=F32)


def upright(total):
    count = total.shape[1]
    row, column = (lax.broadcasted_iota(jnp.int32, (count, count), axis) for axis in range(2))
    total = jnp.concatenate([total.astype(BF16), jnp.zeros((CH, count), BF16)], axis=0)
    return contract((row == column).astype(BF16), total)


def three_taps(value, step):
    return jnp.concatenate([turned(value, -step), value, turned(value, step)], axis=0).astype(BF16)


def tap_rows(total, tap):
    place, e = tap // 3, tap % 3
    tile = slice(LANES * (place // 2), LANES * (place // 2 + 1))
    even = total[CH * e : CH * e + 32, tile]
    odd = total[CH * e + 32 : CH * (e + 1), tile]
    left = lax.broadcasted_iota(jnp.int32, even.shape, 1) < CH
    if place % 2 == 0:
        return jnp.where(left, even, turned(odd, CH))
    return jnp.where(left, turned(even, CH), odd)


def pair_sum(values):
    lane = lax.broadcasted_iota(jnp.int32, values.shape, 1)
    return values + jnp.where(lane % 2 == 0, turned(values, -1), turned(values, 1))


def step_kernel(
    scale,
    nx,
    ny,
    low_ref,
    own_ref,
    high_ref,
    t1_ref,
    t2_ref,
    t2b_ref,
    t3_ref,
    t3b_ref,
    t4_ref,
    t4b_ref,
    out_ref,
    grads_ref,
    f1,
    f2,
    a1,
    p1,
    a2,
    p2,
    sg,
    ci,
    ca,
    cg,
    pg,
    sk,
    g2,
    g3,
    c3,
    g1,
    acc2,
    acc4,
    acc1,
    even,
    odd,
    even1,
    odd1,
):
    wide, tall = nx + 2 * HALO, ny + 2 * HALO

    @pl.loop(0, wide)
    def _(x):
        cells = jnp.concatenate([low_ref[x], own_ref[x], high_ref[x]], axis=0).astype(F32)
        first = lax.broadcasted_iota(jnp.int32, cells.shape, 1) < 4
        before, after = turned(cells, 1), turned(cells, -1)
        top = jnp.where(first, before, pltpu.roll(after, 4, 1))
        f1[x] = jnp.concatenate([top, cells], axis=1).astype(BF16)
        top = jnp.where(first, pltpu.roll(before, 4, 1), after)
        f2[x] = (jnp.concatenate([top, cells], axis=1) * scale).astype(BF16)

    skip_blocks = (ny + 8) // 2

    def skip_product(i):
        return window_row(f2, t4b_ref, 2 * i + 3, 3, skip_blocks)

    def skip_finish(i, product):
        for dx in range(2):
            for y in range(ny + 8):
                sg[2 * i + dx, y] = window_column(product, dx, y)

    lanes = skip_blocks * LANES
    pipelined((nx + 8) // 2, 1, skip_product, skip_finish, even1.at[:, :lanes], odd1.at[:, :lanes])

    def first_product(i):
        return window_row(f1, t1_ref, 2 * i, 0, (ny + 14) // 2)

    def first_finish(i, product):
        for dx in range(2):
            for y in range(ny + 14):
                value = window_column(product, dx, y)
                a1[2 * i + dx, y] = leaky(value).astype(BF16)
                if 0 <= y - 7 < ny:
                    p1[2 * i + dx, y - 7] = value

    pipelined((nx + 14) // 2, 2, first_product, first_finish, even1, odd1)

    pairs = (ny + 12) // 4

    def second_product(t):
        return product_pair(a1, t2_ref, 2 * (t // pairs), 4 * (t % pairs))

    def second_finish(t, product):
        i, j = t // pairs, t % pairs
        for half in range(2):
            total = None
            for dx in range(2):
                for dy in range(2):
                    value = column_of(product, dx, 2 * half + dy, 1)
                    x, y = 2 * i + dx, 4 * j + 2 * half + dy
                    act = leaky(value).astype(BF16)
                    p2[x, y] = value
                    a2[x, y] = act
                    act = act.astype(F32)
                    total = act if total is None else total + act
            ci[i, 2 * j + half] = (pair_sum(total) * 0.125).astype(BF16)

    pipelined((nx + 12) // 2 * pairs, 5, second_product, second_finish, even, odd)

    cx, cy = nx // 2, ny // 2
    coarse_pairs = (cy + 4) // 4

    def coarse_product(t):
        return product_pair(ci, t3_ref, 2 * (t // coarse_pairs), 4 * (t % coarse_pairs))

    def coarse_finish(t, product):
        for dx in range(2):
            for dy in range(4):
                value = column_of(product, dx, dy, 2)
                x, y = 2 * (t // coarse_pairs) + dx, 4 * (t % coarse_pairs) + dy
                ca[x, y] = leaky(value).astype(BF16)
                total = (
                    sg[2 * x, 2 * y]
                    + sg[2 * x, 2 * y + 1]
                    + sg[2 * x + 1, 2 * y]
                    + sg[2 * x + 1, 2 * y + 1]
                )
                cg[x, y] = (pair_sum(total) * slope(value)).astype(BF16)

    pipelined((cx + 4) // 2 * coarse_pairs, 3, coarse_product, coarse_finish, even, odd)

    @pl.loop(0, (cx + 2) // 2)
    def _(i):
        blocks = (cy + 2) // 2
        window = jnp.concatenate([window_of(cg, 2 * i, 2 * j) for j in range(blocks)], axis=1)
        product = jnp.dot(t3b_ref[...], window, preferred_element_type=F32)
        for dx in range(2):
            for dy in range(2 * blocks):
                pg[2 * i + dx, dy] = column_of(product, dx, dy, 2)

    @pl.loop(0, nx + 2)
    def _(x):
        up = (x + 1) // 2
        for y in range(ny + 2):
            right = (y + 1) // 2
            sk[x, y] = (
                a2[x + 5, y + 5].astype(F32) + ca[up + 1, right + 1].astype(F32)
            ).astype(BF16)
            g2[x, y] = (
                (sg[x + 3, y + 3] + pg[up, right] * 0.125) * slope(p2[x + 5, y + 5])
            ).astype(BF16)

    row, column = (lax.broadcasted_iota(jnp.int32, (CH, CH), axis) for axis in range(2))
    parity = (column == 2 * (row % 32) + row // 32).astype(BF16)

    @pl.loop(0, nx)
    def _(x):
        values = jnp.dot(parity, line(g2, x + 1, 1, ny), preferred_element_type=F32)
        for y in range(ny):
            value = values[:, LANES * y : LANES * (y + 1)]
            g3[x, y] = three_taps(value, 1)

    for x in range(cx):
        values = jnp.dot(parity, line(cg, x + 2, 2, cy), preferred_element_type=F32)
        for y in range(cy):
            c3[x, y] = three_taps(values[:, LANES * y : LANES * (y + 1)], 2)

    @pl.loop(0, nx // 2)
    def _(i):
        blocks = ny // 2
        window = jnp.concatenate([window_of(sk, 2 * i, 2 * j) for j in range(blocks)], axis=1)
        product = jnp.dot(t4_ref[...], window, preferred_element_type=F32)
        for dx in range(2):
            for dy in range(ny):
                x = 2 * i + dx
                out_ref[x, dy] = column_of(product, dx, dy, 1) + own_ref[x + HALO, dy].astype(F32)

    fine_pairs = ny // 4

    def back_product(t):
        return product_pair(g2, t2b_ref, 2 * (t // fine_pairs), 4 * (t % fine_pairs))

    def back_finish(t, product):
        for dx in range(2):
            for dy in range(4):
                x, y = 2 * (t // fine_pairs) + dx, 4 * (t % fine_pairs) + dy
                value = column_of(product, dx, dy, 1)
                g1[x, y] = (value * slope(p1[x + 7, y])).astype(BF16)

    pipelined(nx // 2 * fine_pairs, 2, back_product, back_finish, even, odd)

    acc2[...] = jnp.zeros_like(acc2)
    acc4[...] = jnp.zeros_like(acc4)
    acc1[...] = jnp.zeros_like(acc1)

    @pl.loop(0, nx)
    def _(x):
        acc2[...] += contract(
            jnp.concatenate(neighbour_lines(a1, x + 7, 7, ny), axis=0), line(g3, x, 0, ny)
        )
        acc4[...] += contract(
            jnp.concatenate(neighbour_lines(sk, x + 1, 1, ny), axis=0),
            line(f2, x + HALO, HALO, ny),
        )
        acc1[...] += contract(
            jnp.concatenate(neighbour_lines(f1, x + HALO, HALO, ny), axis=0), line(g1, x, 0, ny)
        )

    total3 = 0.5 * sum(
        contract(jnp.concatenate(neighbour_lines(ci, x + 3, 3, cy), axis=0), line(c3, x, 0, cy))
        for x in range(cx)
    )
    total2, total3, total4 = (
        upright(total) for total in (acc2[...], total3, acc4[...])
    )
    for tap in range(27):
        grads_ref[32 * tap : 32 * (tap + 1)] = tap_rows(total2, tap).astype(BF16)
        grads_ref[864 + 32 * tap : 896 + 32 * tap] = tap_rows(total3, tap).astype(BF16)
    for k in range(5):
        grads_ref[1728 + 16 * k : 1744 + 16 * k] = total4[
            :, LANES * k : LANES * (k + 1)
        ].astype(BF16)
    grads_ref[1808:1952] = jnp.concatenate([acc1[...], jnp.zeros_like(acc1)], axis=1).astype(BF16)
    grads_ref[1952:] = jnp.zeros((96, LANES), BF16)


def unpack_kernel(total_ref, two_ref, three_ref, last_ref, first_ref, wide):
    wide[...] = total_ref[:1728].astype(F32)
    for half in range(32):
        lanes = slice(LANES * half, LANES * (half + 1))
        two_ref[:, lanes] = wide[pl.ds(half, 27, stride=32)]
        three_ref[:, lanes] = wide[pl.ds(864 + half, 27, stride=32)]
    for k in range(5):
        last_ref[:, LANES * k : LANES * (k + 1)] = total_ref[
            1728 + 16 * k : 1744 + 16 * k
        ].astype(F32)
    first_ref[...] = total_ref[1808:1952].astype(F32)


def in_vmem(count):
    return [pl.BlockSpec(memory_space=pltpu.VMEM)] * count


def body(field_in, cotangent, kernel_one, kernel_two, kernel_three, kernel_four):
    nx, ny, nz = field_in.shape[1:]
    devices = lax.axis_size("gx") * lax.axis_size("gy")
    scale = 1.0 / math.sqrt(nx * ny * nz * devices)

    blank = jnp.zeros((1, nx, ny, nz), BF16)
    block = jnp.concatenate([field_in, blank, cotangent, blank], axis=0)
    block = jnp.transpose(block, (1, 2, 0, 3))
    block = jnp.concatenate(
        [
            shifted(block, "gx", 2),
            shifted(block, "gx", 1),
            block,
            shifted(block, "gx", -1),
            shifted(block, "gx", -2),
        ],
        axis=0,
    )
    block, kernel_one, kernel_two, kernel_three, kernel_four = lax.optimization_barrier(
        (block, kernel_one, kernel_two, kernel_three, kernel_four)
    )
    blocks = (shifted(block, "gy", 1), block, shifted(block, "gy", -1))

    t2, t2b, t3, t3b = pl.pallas_call(
        weights_kernel,
        out_shape=[jax.ShapeDtypeStruct((6 * CH, 12 * CH), BF16)] * 4,
        in_specs=in_vmem(2),
        out_specs=in_vmem(4),
        cost_estimate=pl.CostEstimate(flops=0, bytes_accessed=30_000_000, transcendentals=0),
    )(kernel_two.reshape(27, CH, CH), kernel_three.reshape(27, CH, CH))
    four = jnp.transpose(kernel_four, (2, 3, 4, 0, 1))
    weights = (
        toeplitz_window(jnp.transpose(kernel_one, (0, 2, 3, 4, 1)), FIELD_ROWS),
        t2,
        t2b,
        t3,
        t3b,
        toeplitz_rows(jnp.pad(four, ((0, 0), (0, 0), (0, 0), (0, 5), (0, 0)))),
        toeplitz_window(jnp.transpose(swapped(four), (3, 0, 1, 2, 4)), GRADIENT_ROWS),
    )

    wide, tall = nx + 2 * HALO, ny + 2 * HALO
    cx, cy = nx // 2, ny // 2

    def fine(more, kind, rows=CH):
        return pltpu.VMEM((nx + 2 * more, ny + 2 * more, rows, LANES), kind)

    def coarse(more, kind, rows=CH):
        return pltpu.VMEM((cx + 2 * more, cy + 2 * more, rows, LANES), kind)

    out, grads = pl.pallas_call(
        lambda *refs: step_kernel(scale, nx, ny, *refs),
        out_shape=[
            jax.ShapeDtypeStruct((nx, ny, 8, LANES), F32),
            jax.ShapeDtypeStruct((2048, LANES), BF16),
        ],
        in_specs=in_vmem(10),
        out_specs=in_vmem(2),
        scratch_shapes=[
            fine(HALO, BF16, 16),
            fine(HALO, BF16, 16),
            fine(7, BF16),
            pltpu.VMEM((nx + 14, ny, CH, LANES), F32),
            fine(6, BF16),
            fine(6, F32),
            fine(4, F32),
            coarse(3, BF16),
            coarse(2, BF16),
            coarse(2, BF16),
            coarse(1, F32),
            fine(1, BF16),
            fine(1, BF16),
            fine(0, BF16, 3 * CH),
            coarse(0, BF16, 3 * CH),
            fine(0, BF16),
            pltpu.VMEM((9 * CH, 3 * CH), F32),
            pltpu.VMEM((9 * CH, 16), F32),
            pltpu.VMEM((144, CH), F32),
            pltpu.VMEM((6 * CH, 4 * LANES), F32),
            pltpu.VMEM((6 * CH, 4 * LANES), F32),
            pltpu.VMEM((4 * CH, (ny + 14) // 2 * LANES), F32),
            pltpu.VMEM((4 * CH, (ny + 14) // 2 * LANES), F32),
        ],
        compiler_params=pltpu.CompilerParams(vmem_limit_bytes=60 * 1024 * 1024),
    )(*blocks, *weights)

    output = jnp.transpose(out[:, :, :3], (2, 0, 1, 3))

    share = lax.all_to_all(grads.reshape(devices, -1, LANES), AXES, 0, 0, tiled=True)
    total = jnp.sum(share.astype(F32), axis=0).astype(BF16)
    total = jnp.broadcast_to(total[None], (devices,) + total.shape)
    total = lax.all_to_all(total, AXES, 0, 0, tiled=True).reshape(2048, LANES)

    grad_two, grad_three, last, first = pl.pallas_call(
        unpack_kernel,
        out_shape=[jax.ShapeDtypeStruct((27, CH * CH), F32)] * 2
        + [
            jax.ShapeDtypeStruct((16, 5 * LANES), F32),
            jax.ShapeDtypeStruct((144, LANES), F32),
        ],
        in_specs=in_vmem(1),
        out_specs=in_vmem(4),
        scratch_shapes=[pltpu.VMEM((1728, LANES), F32)],
    )(total)
    groups = [last[4 * k : 4 * k + 3, : 9 * CH] for k in range(4)]
    taps = [groups[GRADIENT_ROWS.index(2 - e)] for e in range(3)]
    taps = jnp.stack(taps, axis=2).reshape(3, 3, 3, CH, 3)
    grad_four = jnp.transpose(taps, (0, 3, 1, 2, 4))
    first = first[:, :CH].reshape(3, 3, 4, 4, CH)
    taps = jnp.stack([first[:, :, FIELD_ROWS.index(e), :3] for e in range(3)], axis=2)
    grad_one = jnp.transpose(taps, (4, 3, 0, 1, 2))
    return (output, grad_one, grad_two, grad_three, grad_four)


def solution(mesh):
    return jax.shard_map(
        body,
        mesh=mesh,
        in_specs=(P(None, "gx", "gy", None), P(None, "gx", "gy", None), P(), P(), P(), P()),
        out_specs=(P(None, "gx", "gy", None), P(), P(), P(), P()),
        check_vma=False,
    )
```

profile of v0, /device:TPU:1, one launch (start us, length us, event | category | flops | bytes accessed | tf_op | source)
XLA Modules:
  0.0 114.9 jit_solution(4838750772446576807)
XLA Ops:
  0.6 0.8 copy.26
  1.5 0.1 maximum_bitcast_fusion.1
  1.6 3.8 %collective-permute-start = (bf16[4,8,8,128]{3,2,1,0:T(8,128)(2,1)S(1)}, bf16[4,8,8,128]{3,2,1,0:T(8,128)(2,1)S(1)}, u32[]{:S(2)}, u32[]{:S(2)}) collective-permute-start(bf16[4,8,8,128]{3,2,1,0:T(8,128)(2,1)S(1)} %maximum_bitcast_fusion.1), channel_id=1, source_target_pairs={{0,8},{4,12},{8,16},{12,20},{16,24},{20,28},{24,32},{28,36},{32,40... | collective-permute-start | bytes 196616 | tf_op jit(solution)/shard_map/ppermute | solution.py:22
  5.4 0.4 collective-permute-start.1
  5.8 5.3 %collective-permute-start.2 = (bf16[4,8,8,128]{3,2,1,0:T(8,128)(2,1)S(1)}, bf16[4,8,8,128]{3,2,1,0:T(8,128)(2,1)S(1)}, u32[]{:S(2)}, u32[]{:S(2)}) collective-permute-start(bf16[4,8,8,128]{3,2,1,0:T(8,128)(2,1)S(1)} %maximum_bitcast_fusion.1), channel_id=1, source_target_pairs={{0,124},{4,0},{8,4},{12,8},{16,12},{20,16},{24,20},{28,24},{32,28}... | collective-permute-start | bytes 196616 | tf_op jit(solution)/shard_map/ppermute | solution.py:22
  11.1 0.9 collective-permute-start.3
  12.0 1.1 collective-permute-done.1
  13.0 0.1 constant_dynamic-update-slice_fusion.2
  13.1 0.0 collective-permute-done.2
  13.2 0.0 copy-start.8
  13.2 2.5 %collective-permute-done.3 = bf16[4,8,8,128]{3,2,1,0:T(8,128)(2,1)S(1)} collective-permute-done((bf16[4,8,8,128]{3,2,1,0:T(8,128)(2,1)S(1)}, bf16[4,8,8,128]{3,2,1,0:T(8,128)(2,1)S(1)}, u32[]{:S(2)}, u32[]{:S(2)}) %collective-permute-start.3) | collective-permute-done | bytes 65568 | tf_op jit(solution)/shard_map/ppermute | solution.py:22
  15.8 0.0 copy-start.9
  15.8 5.4 %collective-permute-start.4 = (bf16[20,8,8,128]{3,2,1,0:T(8,128)(2,1)S(1)}, bf16[20,8,8,128]{3,2,1,0:T(8,128)(2,1)S(1)}, u32[]{:S(2)}, u32[]{:S(2)}) collective-permute-start(bf16[20,8,8,128]{3,2,1,0:T(8,128)(2,1)S(1)} %constant_dynamic-update-slice_fusion.refs_1_), channel_id=1, source_target_pairs={{0,1},{1,2},{2,3},{3,0},{4,5},{5,6},{6,7},{7,4},{8,9},{9,10},{10,1... | collective-permute-start | bytes 983048 | tf_op jit(solution)/shard_map/ppermute | solution.py:22
  21.2 0.1 pad_maximum_fusion.3
  21.3 0.1 pad_bitcast_fusion.5
  21.4 0.1 pad_maximum_fusion.1
  21.5 0.2 copy.32
  21.7 0.2 reshape.46
  21.9 0.8 copy.34.refs_9_
  22.7 0.1 pad_maximum_fusion
  22.7 0.2 copy.29
  23.0 0.2 reshape.42
  23.2 0.8 copy.33.refs_3_
  24.0 0.0 copy-start.4
  24.0 0.1 copy.31
  24.1 0.8 reshape.45.refs_8_
  24.9 0.1 copy-done.4
  25.0 1.2 %reshape.43.two_ref = bf16[27,64,64]{2,1,0:T(8,128)(2,1)} reshape(bf16[27,4096]{1,0:T(8,128)(2,1)S(1)} %copy-done.4) | data formatting | bytes 442368 | tf_op jit(solution)/shard_map/reshape | solution.py:443
  26.2 1.2 %reshape.44.three_ref = bf16[27,64,64]{2,1,0:T(8,128)(2,1)} reshape(bf16[27,4096]{1,0:T(8,128)(2,1)S(1)} %copy-done.5) | data formatting | bytes 442368 | tf_op jit(solution)/shard_map/reshape | solution.py:443
  27.4 3.7 %shard_map.101 = (bf16[384,768]{1,0:T(8,128)(2,1)}, bf16[384,768]{1,0:T(8,128)(2,1)}, bf16[384,768]{1,0:T(8,128)(2,1)}, bf16[384,768]{1,0:T(8,128)(2,1)}) custom-call(bf16[27,64,64]{2,1,0:T(8,128)(2,1)} %reshape.43.two_ref, bf16[27,64,64]{2,1,0:T(8,128)(2,1)} %reshape.44.three_ref), custom_call_target="tpu_custom_call" | custom-call | bytes 30000000 | tf_op jit(solution)/shard_map/pallas_call | solution.py:437
  31.2 0.7 copy-done.2
  31.9 0.1 copy-done.3
  32.0 36.6 %shard_map.102 = (f32[4,8,8,128]{3,2,1,0:T(8,128)}, bf16[2048,128]{1,0:T(8,128)(2,1)}) custom-call(bf16[20,8,8,128]{3,2,1,0:T(8,128)(2,1)} %copy-done.2, bf16[20,8,8,128]{3,2,1,0:T(8,128)(2,1)} %copy-done.1, bf16[20,8,8,128]{3,2,1,0:T(8,128)(2,1)} %copy-done.3, bf16[256,256]{1,0:T(8,128)(2,1)} %copy.33.refs_3_, bf16[384,768]{1,0:T(8,128)(2,1)} %get-tuple-element.24.refs_4_, ...), custom_call_target="tpu_custom_call" | custom-call | tf_op jit(solution)/shard_map/pallas_call | solution.py:464
  68.6 21.4 %all_to_all.10 = bf16[128,16,128]{2,1,0:T(8,128)(2,1)S(1)} all-to-all(bf16[128,16,128]{2,1,0:T(8,128)(2,1)} %bitcast.61), channel_id=1, replica_groups=mesh['gx'=32,'gy'=4] {'gx','gy'}, dimensions={0} | all-to-all | bytes 1048576 | tf_op jit(solution)/shard_map/all_to_all | solution.py:502
  90.0 0.1 reduce_sum.12
  90.1 0.9 broadcast_in_dim.10
  91.0 4.0 %all-to-all-start.1 = ((bf16[128,16,128]{2,1,0:T(8,128)(2,1)}), bf16[128,16,128]{2,1,0:T(8,128)(2,1)S(1)}, u32[]{:S(2)}, u32[]{:S(2)}) async-start(bf16[128,16,128]{2,1,0:T(8,128)(2,1)} %broadcast_in_dim.10), calls=%async_computation.1 | async-start | bytes 1048576 | tf_op jit(solution)/shard_map/all_to_all | solution.py:505
  95.0 0.6 copy.38
  95.6 13.3 %all-to-all-done.1 = bf16[128,16,128]{2,1,0:T(8,128)(2,1)S(1)} async-done(((bf16[128,16,128]{2,1,0:T(8,128)(2,1)}), bf16[128,16,128]{2,1,0:T(8,128)(2,1)S(1)}, u32[]{:S(2)}, u32[]{:S(2)}) %all-to-all-start.1) | async-done | bytes 524320 | tf_op jit(solution)/shard_map/all_to_all | solution.py:505
  109.0 0.8 copy-done
  109.7 2.5 %shard_map.103 = (f32[27,4096]{1,0:T(8,128)}, f32[27,4096]{1,0:T(8,128)}, f32[16,640]{1,0:T(8,128)}, f32[144,128]{1,0:T(8,128)}) custom-call(bf16[2048,128]{1,0:T(8,128)(2,1)} %bitcast.60), custom_call_target="tpu_custom_call" | custom-call | tf_op jit(solution)/shard_map/pallas_call | solution.py:507
  112.2 0.8 fusion.7
  113.0 0.1 stack.68
  113.1 0.1 stack.69
  113.2 0.1 stack.70
  113.3 0.6 copy.39
  113.9 0.2 copy-done.6
  114.3 0.7 maximum_bitcast_fusion.2
  (39 shorter events, 0.4 us)
Async XLA Ops:
  0.6 0.8 copy-start.10
  1.6 10.4 %collective-permute-start = (bf16[4,8,8,128]{3,2,1,0:T(8,128)(2,1)S(1)}, bf16[4,8,8,128]{3,2,1,0:T(8,128)(2,1)S(1)}, u32[]{:S(2)}, u32[]{:S(2)}) collective-permute-start(bf16[4,8,8,128]{3,2,1,0:T(8,128)(2,1)S(1)} %maximum_bitcast_fusion.1), channel_id=1, source_target_pairs={{0,8},{4,12},{8,16},{12,20},{16,24},{20,28},{24,32},{28,36},{32,40... | collective-permute-start | bytes 196616 | tf_op jit(solution)/shard_map/ppermute | solution.py:22
  5.4 7.7 %collective-permute-start.1 = (bf16[4,8,8,128]{3,2,1,0:T(8,128)(2,1)S(1)}, bf16[4,8,8,128]{3,2,1,0:T(8,128)(2,1)S(1)}, u32[]{:S(2)}, u32[]{:S(2)}) collective-permute-start(bf16[4,8,8,128]{3,2,1,0:T(8,128)(2,1)S(1)} %maximum_bitcast_fusion.1), channel_id=1, source_target_pairs={{0,4},{4,8},{8,12},{12,16},{16,20},{20,24},{24,28},{28,32},{32,36}... | collective-permute-start | bytes 196616 | tf_op jit(solution)/shard_map/ppermute | solution.py:22
  5.8 7.4 %collective-permute-start.2 = (bf16[4,8,8,128]{3,2,1,0:T(8,128)(2,1)S(1)}, bf16[4,8,8,128]{3,2,1,0:T(8,128)(2,1)S(1)}, u32[]{:S(2)}, u32[]{:S(2)}) collective-permute-start(bf16[4,8,8,128]{3,2,1,0:T(8,128)(2,1)S(1)} %maximum_bitcast_fusion.1), channel_id=1, source_target_pairs={{0,124},{4,0},{8,4},{12,8},{16,12},{20,16},{24,20},{28,24},{32,28}... | collective-permute-start | bytes 196616 | tf_op jit(solution)/shard_map/ppermute | solution.py:22
  11.1 4.6 %collective-permute-start.3 = (bf16[4,8,8,128]{3,2,1,0:T(8,128)(2,1)S(1)}, bf16[4,8,8,128]{3,2,1,0:T(8,128)(2,1)S(1)}, u32[]{:S(2)}, u32[]{:S(2)}) collective-permute-start(bf16[4,8,8,128]{3,2,1,0:T(8,128)(2,1)S(1)} %maximum_bitcast_fusion.1), channel_id=1, source_target_pairs={{0,120},{4,124},{8,0},{12,4},{16,8},{20,12},{24,16},{28,20},{32,24... | collective-permute-start | bytes 196616 | tf_op jit(solution)/shard_map/ppermute | solution.py:22
  13.2 2.5 %copy-start.8 = (bf16[3,64,3,3,3]{1,4,3,2,0:T(4,128)(2,1)S(1)}, bf16[3,64,3,3,3]{1,4,3,2,0:T(4,128)(2,1)}, u32[]{:S(2)}) copy-start(bf16[3,64,3,3,3]{1,4,3,2,0:T(4,128)(2,1)} %param.11) | copy-start | bytes 31108
  15.7 5.7 %copy-start.1 = (bf16[20,8,8,128]{3,2,1,0:T(8,128)(2,1)}, bf16[20,8,8,128]{3,2,1,0:T(8,128)(2,1)S(1)}, u32[]{:S(2)}) copy-start(bf16[20,8,8,128]{3,2,1,0:T(8,128)(2,1)S(1)} %constant_dynamic-update-slice_fusion.refs_1_) | copy-start | bytes 983044
  15.8 5.4 %copy-start.9 = (bf16[64,3,3,3,3]{0,4,3,2,1:T(4,128)(2,1)S(1)}, bf16[64,3,3,3,3]{0,4,3,2,1:T(4,128)(2,1)}, u32[]{:S(2)}) copy-start(bf16[64,3,3,3,3]{0,4,3,2,1:T(4,128)(2,1)} %param.8) | copy-start | bytes 31108
  15.8 15.4 %collective-permute-start.4 = (bf16[20,8,8,128]{3,2,1,0:T(8,128)(2,1)S(1)}, bf16[20,8,8,128]{3,2,1,0:T(8,128)(2,1)S(1)}, u32[]{:S(2)}, u32[]{:S(2)}) collective-permute-start(bf16[20,8,8,128]{3,2,1,0:T(8,128)(2,1)S(1)} %constant_dynamic-update-slice_fusion.refs_1_), channel_id=1, source_target_pairs={{0,1},{1,2},{2,3},{3,0},{4,5},{5,6},{6,7},{7,4},{8,9},{9,10},{10,1... | collective-permute-start | bytes 983048 | tf_op jit(solution)/shard_map/ppermute | solution.py:22
  21.1 10.0 %collective-permute-start.5 = (bf16[20,8,8,128]{3,2,1,0:T(8,128)(2,1)S(1)}, bf16[20,8,8,128]{3,2,1,0:T(8,128)(2,1)S(1)}, u32[]{:S(2)}, u32[]{:S(2)}) collective-permute-start(bf16[20,8,8,128]{3,2,1,0:T(8,128)(2,1)S(1)} %constant_dynamic-update-slice_fusion.refs_1_), channel_id=1, source_target_pairs={{0,3},{1,0},{2,1},{3,2},{4,7},{5,4},{6,5},{7,6},{8,11},{9,8},{10,9... | collective-permute-start | bytes 983048 | tf_op jit(solution)/shard_map/ppermute | solution.py:22
  24.0 1.0 copy-start.4
  25.0 1.2 %copy-start.5 = (bf16[27,4096]{1,0:T(8,128)(2,1)S(1)}, bf16[27,4096]{1,0:T(8,128)(2,1)}, u32[]{:S(2)}) copy-start(bf16[27,4096]{1,0:T(8,128)(2,1)} %param.10) | copy-start | bytes 663556
  31.2 0.7 copy-start.2
  31.2 0.8 copy-start.3
  91.0 4.0 %copy-start.7 = (f32[4,8,8,128]{3,2,1,0:T(8,128)S(1)}, f32[4,8,8,128]{3,2,1,0:T(8,128)}, u32[]{:S(2)}) copy-start(f32[4,8,8,128]{3,2,1,0:T(8,128)} %get-tuple-element.29) | copy-start | bytes 393220
  91.0 17.9 %all-to-all-start.1 = ((bf16[128,16,128]{2,1,0:T(8,128)(2,1)}), bf16[128,16,128]{2,1,0:T(8,128)(2,1)S(1)}, u32[]{:S(2)}, u32[]{:S(2)}) async-start(bf16[128,16,128]{2,1,0:T(8,128)(2,1)} %broadcast_in_dim.10), calls=%async_computation.1 | async-start | bytes 1048576 | tf_op jit(solution)/shard_map/all_to_all | solution.py:505
  108.9 0.8 copy-start
  113.3 0.9 copy-start.6
where the time goes:
time: 115 us
  Pallas kernels  42.8 us (37%)
  blocking collectives  21.4 us (19%)
  starting transfers between devices  19.7 us (17%)
  waiting for transfers between devices  16.9 us (15%)
  local copies, waits for them, and re-layouts  11.9 us (10%)
  other arithmetic  1.26 us (1%)
    pallas_call x1, Pallas kernels, body(): pl.pallas_call(lambda *refs: step_kernel(scale, nx, ny, *refs), out_shape...  36.6 us
    all_to_all x1, blocking collectives, body(): lax.all_to_all(grads.reshape(devices, -1, LANES), AXES, 0, 0, tiled=True)  21.4 us
    ppermute x6, starting transfers between devices, shifted(): lax.ppermute(block, axis, [(i, (i + steps) % count) for i in range(count)])  15.8 us
    all_to_all x1, waiting for transfers between devices, body(): total = lax.all_to_all(total, AXES, 0, 0, tiled=True).reshape(2048, LANES)  13.3 us
    unnamed x32, local copies, waits for them, and re-layouts  4.11 us
    all_to_all x1, starting transfers between devices, body(): total = lax.all_to_all(total, AXES, 0, 0, tiled=True).reshape(2048, LANES)  3.97 us
    pallas_call x1, Pallas kernels, body(): pl.pallas_call(weights_kernel, out_shape=[jax.ShapeDtypeStruct((6 * CH, 1...  3.74 us
    ppermute x6, waiting for transfers between devices, shifted(): lax.ppermute(block, axis, [(i, (i + steps) % count) for i in range(count)])  3.56 us
  transfers between devices with their start and end apart: 7, of which 3 were waited for; matrix products, arithmetic and copies ran while one was open for 6% of the time, Pallas kernels for 3%

commit v1 on v0

--- a/solution.py
+++ b/solution.py
@@ -181,17 +181,18 @@
     scale,
     nx,
     ny,
-    low_ref,
+    below2_ref,
+    below1_ref,
     own_ref,
-    high_ref,
+    above1_ref,
+    above2_ref,
     t1_ref,
     t2_ref,
     t2b_ref,
     t3_ref,
     t3b_ref,
-    t4_ref,
     t4b_ref,
-    out_ref,
+    sk,
     grads_ref,
     f1,
     f2,
@@ -204,7 +205,6 @@
     ca,
     cg,
     pg,
-    sk,
     g2,
     g3,
     c3,
@@ -219,15 +219,19 @@
 ):
     wide, tall = nx + 2 * HALO, ny + 2 * HALO
 
-    @pl.loop(0, wide)
-    def _(x):
-        cells = jnp.concatenate([low_ref[x], own_ref[x], high_ref[x]], axis=0).astype(F32)
-        first = lax.broadcasted_iota(jnp.int32, cells.shape, 1) < 4
-        before, after = turned(cells, 1), turned(cells, -1)
-        top = jnp.where(first, before, pltpu.roll(after, 4, 1))
-        f1[x] = jnp.concatenate([top, cells], axis=1).astype(BF16)
-        top = jnp.where(first, pltpu.roll(before, 4, 1), after)
-        f2[x] = (jnp.concatenate([top, cells], axis=1) * scale).astype(BF16)
+    def input_rows(part, first_x):
+        @pl.loop(0, nx, unroll=2)
+        def _(x):
+            cells = part[x].astype(F32)
+            first = lax.broadcasted_iota(jnp.int32, cells.shape, 1) < 4
+            before, after = turned(cells, 1), turned(cells, -1)
+            top = jnp.where(first, before, pltpu.roll(after, 4, 1))
+            f1[x + first_x] = jnp.concatenate([top, cells], axis=1).astype(BF16)
+            top = jnp.where(first, pltpu.roll(before, 4, 1), after)
+            f2[x + first_x] = (jnp.concatenate([top, cells], axis=1) * scale).astype(BF16)
+
+    for k, part in enumerate((below2_ref, below1_ref, own_ref, above1_ref, above2_ref)):
+        input_rows(part, k * nx)
 
     skip_blocks = (ny + 8) // 2
 
@@ -240,7 +244,7 @@
                 sg[2 * i + dx, y] = window_column(product, dx, y)
 
     lanes = skip_blocks * LANES
-    pipelined((nx + 8) // 2, 1, skip_product, skip_finish, even1.at[:, :lanes], odd1.at[:, :lanes])
+    pipelined((nx + 8) // 2, 3, skip_product, skip_finish, even1.at[:, :lanes], odd1.at[:, :lanes])
 
     def first_product(i):
         return window_row(f1, t1_ref, 2 * i, 0, (ny + 14) // 2)
@@ -299,7 +303,7 @@
 
     pipelined((cx + 4) // 2 * coarse_pairs, 3, coarse_product, coarse_finish, even, odd)
 
-    @pl.loop(0, (cx + 2) // 2)
+    @pl.loop(0, (cx + 2) // 2, unroll=True)
     def _(i):
         blocks = (cy + 2) // 2
         window = jnp.concatenate([window_of(cg, 2 * i, 2 * j) for j in range(blocks)], axis=1)
@@ -308,7 +312,7 @@
             for dy in range(2 * blocks):
                 pg[2 * i + dx, dy] = column_of(product, dx, dy, 2)
 
-    @pl.loop(0, nx + 2)
+    @pl.loop(0, nx + 2, unroll=2)
     def _(x):
         up = (x + 1) // 2
         for y in range(ny + 2):
@@ -323,7 +327,7 @@
     row, column = (lax.broadcasted_iota(jnp.int32, (CH, CH), axis) for axis in range(2))
     parity = (column == 2 * (row % 32) + row // 32).astype(BF16)
 
-    @pl.loop(0, nx)
+    @pl.loop(0, nx, unroll=True)
     def _(x):
         values = jnp.dot(parity, line(g2, x + 1, 1, ny), preferred_element_type=F32)
         for y in range(ny):
@@ -334,16 +338,6 @@
         values = jnp.dot(parity, line(cg, x + 2, 2, cy), preferred_element_type=F32)
         for y in range(cy):
             c3[x, y] = three_taps(values[:, LANES * y : LANES * (y + 1)], 2)
-
-    @pl.loop(0, nx // 2)
-    def _(i):
-        blocks = ny // 2
-        window = jnp.concatenate([window_of(sk, 2 * i, 2 * j) for j in range(blocks)], axis=1)
-        product = jnp.dot(t4_ref[...], window, preferred_element_type=F32)
-        for dx in range(2):
-            for dy in range(ny):
-                x = 2 * i + dx
-                out_ref[x, dy] = column_of(product, dx, dy, 1) + own_ref[x + HALO, dy].astype(F32)
 
     fine_pairs = ny // 4
 
@@ -363,7 +357,7 @@
     acc4[...] = jnp.zeros_like(acc4)
     acc1[...] = jnp.zeros_like(acc1)
 
-    @pl.loop(0, nx)
+    @pl.loop(0, nx, unroll=2)
     def _(x):
         acc2[...] += contract(
             jnp.concatenate(neighbour_lines(a1, x + 7, 7, ny), axis=0), line(g3, x, 0, ny)
@@ -394,6 +388,20 @@
     grads_ref[1952:] = jnp.zeros((96, LANES), BF16)
 
 
+def output_kernel(sk, own_ref, t4_ref, out_ref):
+    nx, ny = own_ref.shape[:2]
+
+    @pl.loop(0, nx // 2)
+    def _(i):
+        blocks = ny // 2
+        window = jnp.concatenate([window_of(sk, 2 * i, 2 * j) for j in range(blocks)], axis=1)
+        product = jnp.dot(t4_ref[...], window, preferred_element_type=F32)
+        for dx in range(2):
+            for y in range(ny):
+                x = 2 * i + dx
+                out_ref[x, y] = column_of(product, dx, y, 1) + own_ref[x, y].astype(F32)
+
+
 def unpack_kernel(total_ref, two_ref, three_ref, last_ref, first_ref, wide):
     wide[...] = total_ref[:1728].astype(F32)
     for half in range(32):
@@ -418,21 +426,14 @@
 
     blank = jnp.zeros((1, nx, ny, nz), BF16)
     block = jnp.concatenate([field_in, blank, cotangent, blank], axis=0)
-    block = jnp.transpose(block, (1, 2, 0, 3))
-    block = jnp.concatenate(
-        [
-            shifted(block, "gx", 2),
-            shifted(block, "gx", 1),
-            block,
-            shifted(block, "gx", -1),
-            shifted(block, "gx", -2),
-        ],
-        axis=0,
-    )
-    block, kernel_one, kernel_two, kernel_three, kernel_four = lax.optimization_barrier(
-        (block, kernel_one, kernel_two, kernel_three, kernel_four)
-    )
-    blocks = (shifted(block, "gy", 1), block, shifted(block, "gy", -1))
+    own = jnp.transpose(block, (1, 2, 0, 3))
+    block = jnp.concatenate([shifted(own, "gy", 1), own, shifted(own, "gy", -1)], axis=1)
+    block, kernel_two, kernel_three = lax.optimization_barrier(
+        (block, kernel_two, kernel_three)
+    )
+    below2, below1 = shifted(block, "gx", 2), shifted(block, "gx", 1)
+    above1, above2 = shifted(block, "gx", -1), shifted(block, "gx", -2)
+    blocks = (below2, below1, block, above1, above2)
 
     t2, t2b, t3, t3b = pl.pallas_call(
         weights_kernel,
@@ -448,7 +449,6 @@
         t2b,
         t3,
         t3b,
-        toeplitz_rows(jnp.pad(four, ((0, 0), (0, 0), (0, 0), (0, 5), (0, 0)))),
         toeplitz_window(jnp.transpose(swapped(four), (3, 0, 1, 2, 4)), GRADIENT_ROWS),
     )
 
@@ -461,13 +461,13 @@
     def coarse(more, kind, rows=CH):
         return pltpu.VMEM((cx + 2 * more, cy + 2 * more, rows, LANES), kind)
 
-    out, grads = pl.pallas_call(
+    skip_sum, grads = pl.pallas_call(
         lambda *refs: step_kernel(scale, nx, ny, *refs),
         out_shape=[
-            jax.ShapeDtypeStruct((nx, ny, 8, LANES), F32),
+            jax.ShapeDtypeStruct((nx + 2, ny + 2, CH, LANES), BF16),
             jax.ShapeDtypeStruct((2048, LANES), BF16),
         ],
-        in_specs=in_vmem(10),
+        in_specs=in_vmem(11),
         out_specs=in_vmem(2),
         scratch_shapes=[
             fine(HALO, BF16, 16),
@@ -482,7 +482,6 @@
             coarse(2, BF16),
             coarse(1, F32),
             fine(1, BF16),
-            fine(1, BF16),
             fine(0, BF16, 3 * CH),
             coarse(0, BF16, 3 * CH),
             fine(0, BF16),
@@ -497,6 +496,16 @@
         compiler_params=pltpu.CompilerParams(vmem_limit_bytes=60 * 1024 * 1024),
     )(*blocks, *weights)
 
+    t4 = toeplitz_rows(jnp.pad(four, ((0, 0), (0, 0), (0, 0), (0, 5), (0, 0))))
+    out = pl.pallas_call(
+        output_kernel,
+        out_shape=jax.ShapeDtypeStruct((nx, ny, 8, LANES), F32),
+        in_specs=in_vmem(3),
+        out_specs=in_vmem(1)[0],
+        cost_estimate=pl.CostEstimate(
+            flops=2 * 48 * 12 * CH * nx * ny * LANES // 2, bytes_accessed=2_000_000, transcendentals=0
+        ),
+    )(skip_sum, own, t4)
     output = jnp.transpose(out[:, :, :3], (2, 0, 1, 3))
 
     share = lax.all_to_all(grads.reshape(devices, -1, LANES), AXES, 0, 0, tiled=True)

time: 115 us -> 113 us (0.983)
  blocking collectives: 21.4 us -> 25.9 us
  waiting for transfers between devices: 16.9 us -> 13 us
  starting transfers between devices: 19.7 us -> 16.8 us
  local copies, waits for them, and re-layouts: 11.9 us -> 13.3 us
  Pallas kernels: 42.8 us -> 41.6 us
    all_to_all x1, waiting for transfers between devices: 13.3 us -> 8.54 us  [body(): total = lax.all_to_all(total, AXES, 0, 0, tiled=True).reshape(2048, LANES)]
    all_to_all x1, blocking collectives: 21.4 us -> 25.9 us  [body(): lax.all_to_all(grads.reshape(devices, -1, LANES), AXES, 0, 0, tiled=True)]
    pallas_call x1, Pallas kernels: 36.6 us -> 32.6 us  [body(): pl.pallas_call(lambda *refs: step_kernel(scale, nx, ny, *refs), out_shape...]
    ppermute x6, starting transfers between devices: 15.8 us -> 12.9 us  [shifted(): lax.ppermute(block, axis, [(i, (i + steps) % count) for i in range(count)])]
    pallas_call x0 -> x1, Pallas kernels: none -> 2.83 us  [body(): pl.pallas_call(output_kernel, out_shape=jax.ShapeDtypeStruct((nx, ny, 8,...]
    unnamed x32 -> x35, local copies, waits for them, and re-layouts: 4.11 us -> 4.59 us
  transfers between devices with their start and end apart: 7 -> 7, of which waited for: 3 -> 4; matrix products, arithmetic and copies ran while one was open for 6% -> 7% of each run, Pallas kernels for 3% -> 6%
where the time goes in v1:
time: 113 us
  Pallas kernels  41.6 us (37%)
  blocking collectives  25.9 us (23%)
  starting transfers between devices  16.8 us (15%)
  local copies, waits for them, and re-layouts  13.3 us (12%)
  waiting for transfers between devices  13 us (12%)
  other arithmetic  1.18 us (1%)
    pallas_call x1, Pallas kernels, body(): pl.pallas_call(lambda *refs: step_kernel(scale, nx, ny, *refs), out_shape...  32.6 us
    all_to_all x1, blocking collectives, body(): lax.all_to_all(grads.reshape(devices, -1, LANES), AXES, 0, 0, tiled=True)  25.9 us
    ppermute x6, starting transfers between devices, shifted(): lax.ppermute(block, axis, [(i, (i + steps) % count) for i in range(count)])  12.9 us
    all_to_all x1, waiting for transfers between devices, body(): total = lax.all_to_all(total, AXES, 0, 0, tiled=True).reshape(2048, LANES)  8.54 us
    unnamed x35, local copies, waits for them, and re-layouts  4.59 us
    ppermute x6, waiting for transfers between devices, shifted(): lax.ppermute(block, axis, [(i, (i + steps) % count) for i in range(count)])  4.44 us
    all_to_all x1, starting transfers between devices, body(): total = lax.all_to_all(total, AXES, 0, 0, tiled=True).reshape(2048, LANES)  3.97 us
    pallas_call x1, Pallas kernels, body(): pl.pallas_call(weights_kernel, out_shape=[jax.ShapeDtypeStruct((6 * CH, 1...  3.68 us
  transfers between devices with their start and end apart: 7, of which 4 were waited for; matrix products, arithmetic and copies ran while one was open for 7% of the time, Pallas kernels for 6%

profile of v1, /device:TPU:1, one launch (start us, length us, event | category | flops | bytes accessed | tf_op | source)
XLA Modules:
  0.0 112.8 jit_solution(11316080913529318165)
XLA Ops:
  0.6 0.8 copy.26
  1.5 0.1 maximum_bitcast_fusion.1.own_ref
  1.6 4.2 %collective-permute-start = (bf16[4,8,8,128]{3,2,1,0:T(8,128)(2,1)S(1)}, bf16[4,8,8,128]{3,2,1,0:T(8,128)(2,1)S(1)}, u32[]{:S(2)}, u32[]{:S(2)}) collective-permute-start(bf16[4,8,8,128]{3,2,1,0:T(8,128)(2,1)S(1)} %maximum_bitcast_fusion.1.own_ref), channel_id=1, source_target_pairs={{0,1},{1,2},{2,3},{3,0},{4,5},{5,6},{6,7},{7,4},{8,9},{9,10},{10,1... | collective-permute-start | bytes 196616 | tf_op jit(solution)/shard_map/ppermute | solution.py:22
  5.8 0.0 copy-start.11
  5.9 0.7 copy-done.11
  6.6 0.1 pad_maximum_fusion.4
  6.7 0.1 pad_bitcast_fusion.5
  6.8 0.3 collective-permute-done
  7.1 3.9 %collective-permute-done.1 = bf16[4,8,8,128]{3,2,1,0:T(8,128)(2,1)S(1)} collective-permute-done((bf16[4,8,8,128]{3,2,1,0:T(8,128)(2,1)S(1)}, bf16[4,8,8,128]{3,2,1,0:T(8,128)(2,1)S(1)}, u32[]{:S(2)}, u32[]{:S(2)}) %collective-permute-start.1) | collective-permute-done | bytes 65568 | tf_op jit(solution)/shard_map/ppermute | solution.py:22
  11.0 3.0 %collective-permute-start.2 = (bf16[4,24,8,128]{3,2,1,0:T(8,128)(2,1)S(1)}, bf16[4,24,8,128]{3,2,1,0:T(8,128)(2,1)S(1)}, u32[]{:S(2)}, u32[]{:S(2)}) collective-permute-start(bf16[4,24,8,128]{3,2,1,0:T(8,128)(2,1)S(1)} %pad_maximum_fusion.2.refs_2_), channel_id=1, source_target_pairs={{0,8},{4,12},{8,16},{12,20},{16,24},{20,28},{24,32},{28,36},{32,40... | collective-permute-start | bytes 589832 | tf_op jit(solution)/shard_map/ppermute | solution.py:22
  14.0 0.4 collective-permute-start.3
  14.4 5.3 %collective-permute-start.4 = (bf16[4,24,8,128]{3,2,1,0:T(8,128)(2,1)S(1)}, bf16[4,24,8,128]{3,2,1,0:T(8,128)(2,1)S(1)}, u32[]{:S(2)}, u32[]{:S(2)}) collective-permute-start(bf16[4,24,8,128]{3,2,1,0:T(8,128)(2,1)S(1)} %pad_maximum_fusion.2.refs_2_), channel_id=1, source_target_pairs={{0,124},{4,0},{8,4},{12,8},{16,12},{20,16},{24,20},{28,24},{32,28}... | collective-permute-start | bytes 589832 | tf_op jit(solution)/shard_map/ppermute | solution.py:22
  19.7 0.1 pad_maximum_fusion.1
  19.8 0.2 copy.31
  20.0 0.2 reshape.45
  20.2 0.8 copy.33.refs_10_
  21.0 0.1 pad_maximum_fusion
  21.0 0.2 copy.29
  21.3 0.2 reshape.42
  21.5 0.8 copy.32.refs_5_
  22.3 1.2 %reshape.43.two_ref = bf16[27,64,64]{2,1,0:T(8,128)(2,1)} reshape(bf16[27,4096]{1,0:T(8,128)(2,1)S(1)} %copy-done.3) | data formatting | bytes 442368 | tf_op jit(solution)/shard_map/reshape | solution.py:444
  23.5 1.2 %reshape.44.three_ref = bf16[27,64,64]{2,1,0:T(8,128)(2,1)} reshape(bf16[27,4096]{1,0:T(8,128)(2,1)S(1)} %copy-done.4) | data formatting | bytes 442368 | tf_op jit(solution)/shard_map/reshape | solution.py:444
  24.7 3.7 %shard_map.101 = (bf16[384,768]{1,0:T(8,128)(2,1)}, bf16[384,768]{1,0:T(8,128)(2,1)}, bf16[384,768]{1,0:T(8,128)(2,1)}, bf16[384,768]{1,0:T(8,128)(2,1)}) custom-call(bf16[27,64,64]{2,1,0:T(8,128)(2,1)} %reshape.43.two_ref, bf16[27,64,64]{2,1,0:T(8,128)(2,1)} %reshape.44.three_ref), custom_call_target="tpu_custom_call" | custom-call | bytes 30000000 | tf_op jit(solution)/shard_map/pallas_call | solution.py:438
  28.4 0.2 collective-permute-done.5.refs_4_
  28.7 0.4 copy-done.5
  29.1 0.1 copy-done.6
  29.1 0.1 copy-done.7
  29.2 0.2 copy-done.8
  29.4 32.6 %shard_map.102 = (bf16[6,10,64,128]{3,2,1,0:T(8,128)(2,1)}, bf16[2048,128]{1,0:T(8,128)(2,1)}) custom-call(bf16[4,24,8,128]{3,2,1,0:T(8,128)(2,1)} %copy-done.5, bf16[4,24,8,128]{3,2,1,0:T(8,128)(2,1)} %copy-done.6, bf16[4,24,8,128]{3,2,1,0:T(8,128)(2,1)} %copy-done.1, bf16[4,24,8,128]{3,2,1,0:T(8,128)(2,1)} %copy-done.7, bf16[4,24,8,128]{3,2,1,0:T(8,128)(2,1)} %copy-done.8, ...), custom_call_target="tpu_custom_call" | custom-call | tf_op jit(solution)/shard_map/pallas_call | solution.py:464
  62.0 25.9 %all_to_all.10 = bf16[128,16,128]{2,1,0:T(8,128)(2,1)S(1)} all-to-all(bf16[128,16,128]{2,1,0:T(8,128)(2,1)} %bitcast.59), channel_id=1, replica_groups=mesh['gx'=32,'gy'=4] {'gx','gy'}, dimensions={0} | all-to-all | bytes 1048576 | tf_op jit(solution)/shard_map/all_to_all | solution.py:511
  87.9 0.1 reduce_sum.12
  88.1 0.9 broadcast_in_dim.10
  89.0 4.0 %all-to-all-start.1 = ((bf16[128,16,128]{2,1,0:T(8,128)(2,1)}), bf16[128,16,128]{2,1,0:T(8,128)(2,1)S(1)}, u32[]{:S(2)}, u32[]{:S(2)}) async-start(bf16[128,16,128]{2,1,0:T(8,128)(2,1)} %broadcast_in_dim.10), calls=%async_computation.1 | async-start | bytes 1048576 | tf_op jit(solution)/shard_map/all_to_all | solution.py:514
  93.0 0.1 copy.34
  93.1 0.8 reshape.46.t4_ref
  93.9 2.8 %shard_map.103 = f32[4,8,8,128]{3,2,1,0:T(8,128)} custom-call(bf16[6,10,64,128]{3,2,1,0:T(8,128)(2,1)} %get-tuple-element.25.sk, bf16[4,8,8,128]{3,2,1,0:T(8,128)(2,1)} %copy-done.2, bf16[48,768]{1,0:T(8,128)(2,1)} %reshape.46.t4_ref), custom_call_target="tpu_custom_call" | custom-call | flops 150994944 | bytes 2000000 | tf_op jit(solution)/shard_map/pallas_call | solution.py:500
  96.7 0.9 slice_bitcast_fusion
  97.6 0.6 copy.38
  98.2 8.5 %all-to-all-done.1 = bf16[128,16,128]{2,1,0:T(8,128)(2,1)S(1)} async-done(((bf16[128,16,128]{2,1,0:T(8,128)(2,1)}), bf16[128,16,128]{2,1,0:T(8,128)(2,1)S(1)}, u32[]{:S(2)}, u32[]{:S(2)}) %all-to-all-start.1) | async-done | bytes 524320 | tf_op jit(solution)/shard_map/all_to_all | solution.py:514
  106.8 0.8 copy-done
  107.6 2.4 %shard_map.104 = (f32[27,4096]{1,0:T(8,128)}, f32[27,4096]{1,0:T(8,128)}, f32[16,640]{1,0:T(8,128)}, f32[144,128]{1,0:T(8,128)}) custom-call(bf16[2048,128]{1,0:T(8,128)(2,1)} %bitcast.58), custom_call_target="tpu_custom_call" | custom-call | tf_op jit(solution)/shard_map/pallas_call | solution.py:516
  110.0 0.8 fusion.7
  110.8 0.1 stack.68
  110.9 0.1 stack.69
  111.0 0.1 stack.70
  111.1 0.6 copy.39
  111.8 0.2 copy-done.9
  112.1 0.7 maximum_bitcast_fusion.2
  (40 shorter events, 0.3 us)
Async XLA Ops:
  0.6 0.8 copy-start.12
  1.5 4.3 %copy-start.10 = (bf16[3,64,3,3,3]{1,4,3,2,0:T(4,128)(2,1)S(1)}, bf16[3,64,3,3,3]{1,4,3,2,0:T(4,128)(2,1)}, u32[]{:S(2)}) copy-start(bf16[3,64,3,3,3]{1,4,3,2,0:T(4,128)(2,1)} %param.11) | copy-start | bytes 31108
  1.6 9.4 %copy-start.2 = (bf16[4,8,8,128]{3,2,1,0:T(8,128)(2,1)}, bf16[4,8,8,128]{3,2,1,0:T(8,128)(2,1)S(1)}, u32[]{:S(2)}) copy-start(bf16[4,8,8,128]{3,2,1,0:T(8,128)(2,1)S(1)} %maximum_bitcast_fusion.1.own_ref) | copy-start | bytes 196612
  1.6 5.5 %collective-permute-start = (bf16[4,8,8,128]{3,2,1,0:T(8,128)(2,1)S(1)}, bf16[4,8,8,128]{3,2,1,0:T(8,128)(2,1)S(1)}, u32[]{:S(2)}, u32[]{:S(2)}) collective-permute-start(bf16[4,8,8,128]{3,2,1,0:T(8,128)(2,1)S(1)} %maximum_bitcast_fusion.1.own_ref), channel_id=1, source_target_pairs={{0,1},{1,2},{2,3},{3,0},{4,5},{5,6},{6,7},{7,4},{8,9},{9,10},{10,1... | collective-permute-start | bytes 196616 | tf_op jit(solution)/shard_map/ppermute | solution.py:22
  5.8 5.2 %collective-permute-start.1 = (bf16[4,8,8,128]{3,2,1,0:T(8,128)(2,1)S(1)}, bf16[4,8,8,128]{3,2,1,0:T(8,128)(2,1)S(1)}, u32[]{:S(2)}, u32[]{:S(2)}) collective-permute-start(bf16[4,8,8,128]{3,2,1,0:T(8,128)(2,1)S(1)} %maximum_bitcast_fusion.1.own_ref), channel_id=1, source_target_pairs={{0,3},{1,0},{2,1},{3,2},{4,7},{5,4},{6,5},{7,6},{8,11},{9,8},{10,9... | collective-permute-start | bytes 196616 | tf_op jit(solution)/shard_map/ppermute | solution.py:22
  5.8 0.7 copy-start.11
  11.0 8.8 %copy-start.1 = (bf16[4,24,8,128]{3,2,1,0:T(8,128)(2,1)}, bf16[4,24,8,128]{3,2,1,0:T(8,128)(2,1)S(1)}, u32[]{:S(2)}) copy-start(bf16[4,24,8,128]{3,2,1,0:T(8,128)(2,1)S(1)} %pad_maximum_fusion.2.refs_2_) | copy-start | bytes 589828
  11.0 17.4 %collective-permute-start.2 = (bf16[4,24,8,128]{3,2,1,0:T(8,128)(2,1)S(1)}, bf16[4,24,8,128]{3,2,1,0:T(8,128)(2,1)S(1)}, u32[]{:S(2)}, u32[]{:S(2)}) collective-permute-start(bf16[4,24,8,128]{3,2,1,0:T(8,128)(2,1)S(1)} %pad_maximum_fusion.2.refs_2_), channel_id=1, source_target_pairs={{0,8},{4,12},{8,16},{12,20},{16,24},{20,28},{24,32},{28,36},{32,40... | collective-permute-start | bytes 589832 | tf_op jit(solution)/shard_map/ppermute | solution.py:22
  14.0 14.4 %collective-permute-start.3 = (bf16[4,24,8,128]{3,2,1,0:T(8,128)(2,1)S(1)}, bf16[4,24,8,128]{3,2,1,0:T(8,128)(2,1)S(1)}, u32[]{:S(2)}, u32[]{:S(2)}) collective-permute-start(bf16[4,24,8,128]{3,2,1,0:T(8,128)(2,1)S(1)} %pad_maximum_fusion.2.refs_2_), channel_id=1, source_target_pairs={{0,4},{4,8},{8,12},{12,16},{16,20},{20,24},{24,28},{28,32},{32,36}... | collective-permute-start | bytes 589832 | tf_op jit(solution)/shard_map/ppermute | solution.py:22
  14.4 14.0 %collective-permute-start.4 = (bf16[4,24,8,128]{3,2,1,0:T(8,128)(2,1)S(1)}, bf16[4,24,8,128]{3,2,1,0:T(8,128)(2,1)S(1)}, u32[]{:S(2)}, u32[]{:S(2)}) collective-permute-start(bf16[4,24,8,128]{3,2,1,0:T(8,128)(2,1)S(1)} %pad_maximum_fusion.2.refs_2_), channel_id=1, source_target_pairs={{0,124},{4,0},{8,4},{12,8},{16,12},{20,16},{24,20},{28,24},{32,28}... | collective-permute-start | bytes 589832 | tf_op jit(solution)/shard_map/ppermute | solution.py:22
  19.7 9.0 %collective-permute-start.5 = (bf16[4,24,8,128]{3,2,1,0:T(8,128)(2,1)S(1)}, bf16[4,24,8,128]{3,2,1,0:T(8,128)(2,1)S(1)}, u32[]{:S(2)}, u32[]{:S(2)}) collective-permute-start(bf16[4,24,8,128]{3,2,1,0:T(8,128)(2,1)S(1)} %pad_maximum_fusion.2.refs_2_), channel_id=1, source_target_pairs={{0,120},{4,124},{8,0},{12,4},{16,8},{20,12},{24,16},{28,20},{32,24... | collective-permute-start | bytes 589832 | tf_op jit(solution)/shard_map/ppermute | solution.py:22
  21.3 1.0 copy-start.3
  22.2 1.2 %copy-start.4 = (bf16[27,4096]{1,0:T(8,128)(2,1)S(1)}, bf16[27,4096]{1,0:T(8,128)(2,1)}, u32[]{:S(2)}) copy-start(bf16[27,4096]{1,0:T(8,128)(2,1)} %param.10) | copy-start | bytes 663556
  28.4 0.7 copy-start.5
  28.4 0.7 copy-start.6
  28.4 0.8 copy-start.7
  28.7 0.7 copy-start.8
  89.0 17.8 %all-to-all-start.1 = ((bf16[128,16,128]{2,1,0:T(8,128)(2,1)}), bf16[128,16,128]{2,1,0:T(8,128)(2,1)S(1)}, u32[]{:S(2)}, u32[]{:S(2)}) async-start(bf16[128,16,128]{2,1,0:T(8,128)(2,1)} %broadcast_in_dim.10), calls=%async_computation.1 | async-start | bytes 1048576 | tf_op jit(solution)/shard_map/all_to_all | solution.py:514
  106.8 0.8 copy-start
  111.1 0.9 copy-start.9

commit v2 on v1

--- a/solution.py
+++ b/solution.py
@@ -220,7 +220,7 @@
     wide, tall = nx + 2 * HALO, ny + 2 * HALO
 
     def input_rows(part, first_x):
-        @pl.loop(0, nx, unroll=2)
+        @pl.loop(0, nx, unroll=4)
         def _(x):
             cells = part[x].astype(F32)
             first = lax.broadcasted_iota(jnp.int32, cells.shape, 1) < 4
@@ -257,7 +257,7 @@
                 if 0 <= y - 7 < ny:
                     p1[2 * i + dx, y - 7] = value
 
-    pipelined((nx + 14) // 2, 2, first_product, first_finish, even1, odd1)
+    pipelined((nx + 14) // 2, 4, first_product, first_finish, even1, odd1)
 
     pairs = (ny + 12) // 4
 
@@ -312,7 +312,7 @@
             for dy in range(2 * blocks):
                 pg[2 * i + dx, dy] = column_of(product, dx, dy, 2)
 
-    @pl.loop(0, nx + 2, unroll=2)
+    @pl.loop(0, nx + 2, unroll=3)
     def _(x):
         up = (x + 1) // 2
         for y in range(ny + 2):
@@ -357,7 +357,7 @@
     acc4[...] = jnp.zeros_like(acc4)
     acc1[...] = jnp.zeros_like(acc1)
 
-    @pl.loop(0, nx, unroll=2)
+    @pl.loop(0, nx, unroll=4)
     def _(x):
         acc2[...] += contract(
             jnp.concatenate(neighbour_lines(a1, x + 7, 7, ny), axis=0), line(g3, x, 0, ny)

time: 113 us -> 111 us (0.982)
  Pallas kernels: 41.6 us -> 38.7 us
    pallas_call x1, Pallas kernels: 32.6 us -> 29.8 us  [body(): pl.pallas_call(lambda *refs: step_kernel(scale, nx, ny, *refs), out_shape...]
where the time goes in v2:
time: 111 us; the launch traced here: 110 us
  Pallas kernels  38.7 us (35%)
  blocking collectives  26 us (23%)
  starting transfers between devices  16.8 us (15%)
  local copies, waits for them, and re-layouts  13.3 us (12%)
  waiting for transfers between devices  13 us (12%)
  other arithmetic  1.18 us (1%)
    pallas_call x1, Pallas kernels, body(): pl.pallas_call(lambda *refs: step_kernel(scale, nx, ny, *refs), out_shape...  29.8 us
    all_to_all x1, blocking collectives, body(): lax.all_to_all(grads.reshape(devices, -1, LANES), AXES, 0, 0, tiled=True)  26 us
    ppermute x6, starting transfers between devices, shifted(): lax.ppermute(block, axis, [(i, (i + steps) % count) for i in range(count)])  12.9 us
    all_to_all x1, waiting for transfers between devices, body(): total = lax.all_to_all(total, AXES, 0, 0, tiled=True).reshape(2048, LANES)  8.54 us
    unnamed x35, local copies, waits for them, and re-layouts  4.59 us
    ppermute x6, waiting for transfers between devices, shifted(): lax.ppermute(block, axis, [(i, (i + steps) % count) for i in range(count)])  4.44 us
    all_to_all x1, starting transfers between devices, body(): total = lax.all_to_all(total, AXES, 0, 0, tiled=True).reshape(2048, LANES)  3.97 us
    pallas_call x1, Pallas kernels, body(): pl.pallas_call(weights_kernel, out_shape=[jax.ShapeDtypeStruct((6 * CH, 1...  3.68 us
  transfers between devices with their start and end apart: 7, of which 4 were waited for; matrix products, arithmetic and copies ran while one was open for 7% of the time, Pallas kernels for 6%

profile of v2, /device:TPU:1, one launch (start us, length us, event | category | flops | bytes accessed | tf_op | source)
XLA Modules:
  0.0 109.9 jit_solution(10975974997338793832)
XLA Ops:
  0.6 0.8 copy.26
  1.5 0.1 maximum_bitcast_fusion.1.own_ref
  1.6 4.2 %collective-permute-start = (bf16[4,8,8,128]{3,2,1,0:T(8,128)(2,1)S(1)}, bf16[4,8,8,128]{3,2,1,0:T(8,128)(2,1)S(1)}, u32[]{:S(2)}, u32[]{:S(2)}) collective-permute-start(bf16[4,8,8,128]{3,2,1,0:T(8,128)(2,1)S(1)} %maximum_bitcast_fusion.1.own_ref), channel_id=1, source_target_pairs={{0,1},{1,2},{2,3},{3,0},{4,5},{5,6},{6,7},{7,4},{8,9},{9,10},{10,1... | collective-permute-start | bytes 196616 | tf_op jit(solution)/shard_map/ppermute | solution.py:22
  5.8 0.0 copy-start.11
  5.9 0.7 copy-done.11
  6.6 0.1 pad_maximum_fusion.4
  6.7 0.1 pad_bitcast_fusion.5
  6.8 0.3 collective-permute-done
  7.1 3.9 %collective-permute-done.1 = bf16[4,8,8,128]{3,2,1,0:T(8,128)(2,1)S(1)} collective-permute-done((bf16[4,8,8,128]{3,2,1,0:T(8,128)(2,1)S(1)}, bf16[4,8,8,128]{3,2,1,0:T(8,128)(2,1)S(1)}, u32[]{:S(2)}, u32[]{:S(2)}) %collective-permute-start.1) | collective-permute-done | bytes 65568 | tf_op jit(solution)/shard_map/ppermute | solution.py:22
  11.0 3.0 %collective-permute-start.2 = (bf16[4,24,8,128]{3,2,1,0:T(8,128)(2,1)S(1)}, bf16[4,24,8,128]{3,2,1,0:T(8,128)(2,1)S(1)}, u32[]{:S(2)}, u32[]{:S(2)}) collective-permute-start(bf16[4,24,8,128]{3,2,1,0:T(8,128)(2,1)S(1)} %pad_maximum_fusion.2.refs_2_), channel_id=1, source_target_pairs={{0,8},{4,12},{8,16},{12,20},{16,24},{20,28},{24,32},{28,36},{32,40... | collective-permute-start | bytes 589832 | tf_op jit(solution)/shard_map/ppermute | solution.py:22
  14.0 0.4 collective-permute-start.3
  14.4 5.3 %collective-permute-start.4 = (bf16[4,24,8,128]{3,2,1,0:T(8,128)(2,1)S(1)}, bf16[4,24,8,128]{3,2,1,0:T(8,128)(2,1)S(1)}, u32[]{:S(2)}, u32[]{:S(2)}) collective-permute-start(bf16[4,24,8,128]{3,2,1,0:T(8,128)(2,1)S(1)} %pad_maximum_fusion.2.refs_2_), channel_id=1, source_target_pairs={{0,124},{4,0},{8,4},{12,8},{16,12},{20,16},{24,20},{28,24},{32,28}... | collective-permute-start | bytes 589832 | tf_op jit(solution)/shard_map/ppermute | solution.py:22
  19.7 0.1 pad_maximum_fusion.1
  19.8 0.2 copy.31
  20.0 0.2 reshape.45
  20.2 0.8 copy.33.refs_10_
  21.0 0.1 pad_maximum_fusion
  21.0 0.2 copy.29
  21.3 0.2 reshape.42
  21.5 0.8 copy.32.refs_5_
  22.3 1.2 %reshape.43.two_ref = bf16[27,64,64]{2,1,0:T(8,128)(2,1)} reshape(bf16[27,4096]{1,0:T(8,128)(2,1)S(1)} %copy-done.3) | data formatting | bytes 442368 | tf_op jit(solution)/shard_map/reshape | solution.py:444
  23.5 1.2 %reshape.44.three_ref = bf16[27,64,64]{2,1,0:T(8,128)(2,1)} reshape(bf16[27,4096]{1,0:T(8,128)(2,1)S(1)} %copy-done.4) | data formatting | bytes 442368 | tf_op jit(solution)/shard_map/reshape | solution.py:444
  24.7 3.7 %shard_map.101 = (bf16[384,768]{1,0:T(8,128)(2,1)}, bf16[384,768]{1,0:T(8,128)(2,1)}, bf16[384,768]{1,0:T(8,128)(2,1)}, bf16[384,768]{1,0:T(8,128)(2,1)}) custom-call(bf16[27,64,64]{2,1,0:T(8,128)(2,1)} %reshape.43.two_ref, bf16[27,64,64]{2,1,0:T(8,128)(2,1)} %reshape.44.three_ref), custom_call_target="tpu_custom_call" | custom-call | bytes 30000000 | tf_op jit(solution)/shard_map/pallas_call | solution.py:438
  28.4 0.2 collective-permute-done.5.refs_4_
  28.7 0.4 copy-done.5
  29.1 0.1 copy-done.6
  29.1 0.1 copy-done.7
  29.2 0.2 copy-done.8
  29.4 29.8 %shard_map.102 = (bf16[6,10,64,128]{3,2,1,0:T(8,128)(2,1)}, bf16[2048,128]{1,0:T(8,128)(2,1)}) custom-call(bf16[4,24,8,128]{3,2,1,0:T(8,128)(2,1)} %copy-done.5, bf16[4,24,8,128]{3,2,1,0:T(8,128)(2,1)} %copy-done.6, bf16[4,24,8,128]{3,2,1,0:T(8,128)(2,1)} %copy-done.1, bf16[4,24,8,128]{3,2,1,0:T(8,128)(2,1)} %copy-done.7, bf16[4,24,8,128]{3,2,1,0:T(8,128)(2,1)} %copy-done.8, ...), custom_call_target="tpu_custom_call" | custom-call | tf_op jit(solution)/shard_map/pallas_call | solution.py:464
  59.1 26.0 %all_to_all.10 = bf16[128,16,128]{2,1,0:T(8,128)(2,1)S(1)} all-to-all(bf16[128,16,128]{2,1,0:T(8,128)(2,1)} %bitcast.59), channel_id=1, replica_groups=mesh['gx'=32,'gy'=4] {'gx','gy'}, dimensions={0} | all-to-all | bytes 1048576 | tf_op jit(solution)/shard_map/all_to_all | solution.py:511
  85.1 0.1 reduce_sum.12
  85.2 0.9 broadcast_in_dim.10
  86.1 4.0 %all-to-all-start.1 = ((bf16[128,16,128]{2,1,0:T(8,128)(2,1)}), bf16[128,16,128]{2,1,0:T(8,128)(2,1)S(1)}, u32[]{:S(2)}, u32[]{:S(2)}) async-start(bf16[128,16,128]{2,1,0:T(8,128)(2,1)} %broadcast_in_dim.10), calls=%async_computation.1 | async-start | bytes 1048576 | tf_op jit(solution)/shard_map/all_to_all | solution.py:514
  90.2 0.1 copy.34
  90.2 0.8 reshape.46.t4_ref
  91.0 2.8 %shard_map.103 = f32[4,8,8,128]{3,2,1,0:T(8,128)} custom-call(bf16[6,10,64,128]{3,2,1,0:T(8,128)(2,1)} %get-tuple-element.25.sk, bf16[4,8,8,128]{3,2,1,0:T(8,128)(2,1)} %copy-done.2, bf16[48,768]{1,0:T(8,128)(2,1)} %reshape.46.t4_ref), custom_call_target="tpu_custom_call" | custom-call | flops 150994944 | bytes 2000000 | tf_op jit(solution)/shard_map/pallas_call | solution.py:500
  93.9 0.9 slice_bitcast_fusion
  94.8 0.6 copy.38
  95.4 8.5 %all-to-all-done.1 = bf16[128,16,128]{2,1,0:T(8,128)(2,1)S(1)} async-done(((bf16[128,16,128]{2,1,0:T(8,128)(2,1)}), bf16[128,16,128]{2,1,0:T(8,128)(2,1)S(1)}, u32[]{:S(2)}, u32[]{:S(2)}) %all-to-all-start.1) | async-done | bytes 524320 | tf_op jit(solution)/shard_map/all_to_all | solution.py:514
  103.9 0.8 copy-done
  104.8 2.4 %shard_map.104 = (f32[27,4096]{1,0:T(8,128)}, f32[27,4096]{1,0:T(8,128)}, f32[16,640]{1,0:T(8,128)}, f32[144,128]{1,0:T(8,128)}) custom-call(bf16[2048,128]{1,0:T(8,128)(2,1)} %bitcast.58), custom_call_target="tpu_custom_call" | custom-call | tf_op jit(solution)/shard_map/pallas_call | solution.py:516
  107.2 0.8 fusion.7
  108.0 0.1 stack.68
  108.1 0.1 stack.69
  108.2 0.1 stack.70
  108.3 0.6 copy.39
  108.9 0.2 copy-done.9
  109.3 0.7 maximum_bitcast_fusion.2
  (40 shorter events, 0.3 us)
Async XLA Ops:
  0.6 0.8 copy-start.12
  1.5 4.3 %copy-start.10 = (bf16[3,64,3,3,3]{1,4,3,2,0:T(4,128)(2,1)S(1)}, bf16[3,64,3,3,3]{1,4,3,2,0:T(4,128)(2,1)}, u32[]{:S(2)}) copy-start(bf16[3,64,3,3,3]{1,4,3,2,0:T(4,128)(2,1)} %param.11) | copy-start | bytes 31108
  1.6 9.4 %copy-start.2 = (bf16[4,8,8,128]{3,2,1,0:T(8,128)(2,1)}, bf16[4,8,8,128]{3,2,1,0:T(8,128)(2,1)S(1)}, u32[]{:S(2)}) copy-start(bf16[4,8,8,128]{3,2,1,0:T(8,128)(2,1)S(1)} %maximum_bitcast_fusion.1.own_ref) | copy-start | bytes 196612
  1.6 5.5 %collective-permute-start = (bf16[4,8,8,128]{3,2,1,0:T(8,128)(2,1)S(1)}, bf16[4,8,8,128]{3,2,1,0:T(8,128)(2,1)S(1)}, u32[]{:S(2)}, u32[]{:S(2)}) collective-permute-start(bf16[4,8,8,128]{3,2,1,0:T(8,128)(2,1)S(1)} %maximum_bitcast_fusion.1.own_ref), channel_id=1, source_target_pairs={{0,1},{1,2},{2,3},{3,0},{4,5},{5,6},{6,7},{7,4},{8,9},{9,10},{10,1... | collective-permute-start | bytes 196616 | tf_op jit(solution)/shard_map/ppermute | solution.py:22
  5.8 5.2 %collective-permute-start.1 = (bf16[4,8,8,128]{3,2,1,0:T(8,128)(2,1)S(1)}, bf16[4,8,8,128]{3,2,1,0:T(8,128)(2,1)S(1)}, u32[]{:S(2)}, u32[]{:S(2)}) collective-permute-start(bf16[4,8,8,128]{3,2,1,0:T(8,128)(2,1)S(1)} %maximum_bitcast_fusion.1.own_ref), channel_id=1, source_target_pairs={{0,3},{1,0},{2,1},{3,2},{4,7},{5,4},{6,5},{7,6},{8,11},{9,8},{10,9... | collective-permute-start | bytes 196616 | tf_op jit(solution)/shard_map/ppermute | solution.py:22
  5.8 0.7 copy-start.11
  11.0 8.8 %copy-start.1 = (bf16[4,24,8,128]{3,2,1,0:T(8,128)(2,1)}, bf16[4,24,8,128]{3,2,1,0:T(8,128)(2,1)S(1)}, u32[]{:S(2)}) copy-start(bf16[4,24,8,128]{3,2,1,0:T(8,128)(2,1)S(1)} %pad_maximum_fusion.2.refs_2_) | copy-start | bytes 589828
  11.0 17.4 %collective-permute-start.2 = (bf16[4,24,8,128]{3,2,1,0:T(8,128)(2,1)S(1)}, bf16[4,24,8,128]{3,2,1,0:T(8,128)(2,1)S(1)}, u32[]{:S(2)}, u32[]{:S(2)}) collective-permute-start(bf16[4,24,8,128]{3,2,1,0:T(8,128)(2,1)S(1)} %pad_maximum_fusion.2.refs_2_), channel_id=1, source_target_pairs={{0,8},{4,12},{8,16},{12,20},{16,24},{20,28},{24,32},{28,36},{32,40... | collective-permute-start | bytes 589832 | tf_op jit(solution)/shard_map/ppermute | solution.py:22
  14.0 14.4 %collective-permute-start.3 = (bf16[4,24,8,128]{3,2,1,0:T(8,128)(2,1)S(1)}, bf16[4,24,8,128]{3,2,1,0:T(8,128)(2,1)S(1)}, u32[]{:S(2)}, u32[]{:S(2)}) collective-permute-start(bf16[4,24,8,128]{3,2,1,0:T(8,128)(2,1)S(1)} %pad_maximum_fusion.2.refs_2_), channel_id=1, source_target_pairs={{0,4},{4,8},{8,12},{12,16},{16,20},{20,24},{24,28},{28,32},{32,36}... | collective-permute-start | bytes 589832 | tf_op jit(solution)/shard_map/ppermute | solution.py:22
  14.4 14.0 %collective-permute-start.4 = (bf16[4,24,8,128]{3,2,1,0:T(8,128)(2,1)S(1)}, bf16[4,24,8,128]{3,2,1,0:T(8,128)(2,1)S(1)}, u32[]{:S(2)}, u32[]{:S(2)}) collective-permute-start(bf16[4,24,8,128]{3,2,1,0:T(8,128)(2,1)S(1)} %pad_maximum_fusion.2.refs_2_), channel_id=1, source_target_pairs={{0,124},{4,0},{8,4},{12,8},{16,12},{20,16},{24,20},{28,24},{32,28}... | collective-permute-start | bytes 589832 | tf_op jit(solution)/shard_map/ppermute | solution.py:22
  19.7 9.0 %collective-permute-start.5 = (bf16[4,24,8,128]{3,2,1,0:T(8,128)(2,1)S(1)}, bf16[4,24,8,128]{3,2,1,0:T(8,128)(2,1)S(1)}, u32[]{:S(2)}, u32[]{:S(2)}) collective-permute-start(bf16[4,24,8,128]{3,2,1,0:T(8,128)(2,1)S(1)} %pad_maximum_fusion.2.refs_2_), channel_id=1, source_target_pairs={{0,120},{4,124},{8,0},{12,4},{16,8},{20,12},{24,16},{28,20},{32,24... | collective-permute-start | bytes 589832 | tf_op jit(solution)/shard_map/ppermute | solution.py:22
  21.3 1.0 copy-start.3
  22.2 1.2 %copy-start.4 = (bf16[27,4096]{1,0:T(8,128)(2,1)S(1)}, bf16[27,4096]{1,0:T(8,128)(2,1)}, u32[]{:S(2)}) copy-start(bf16[27,4096]{1,0:T(8,128)(2,1)} %param.10) | copy-start | bytes 663556
  28.4 0.7 copy-start.5
  28.4 0.7 copy-start.6
  28.4 0.8 copy-start.7
  28.7 0.7 copy-start.8
  86.1 17.8 %all-to-all-start.1 = ((bf16[128,16,128]{2,1,0:T(8,128)(2,1)}), bf16[128,16,128]{2,1,0:T(8,128)(2,1)S(1)}, u32[]{:S(2)}, u32[]{:S(2)}) async-start(bf16[128,16,128]{2,1,0:T(8,128)(2,1)} %broadcast_in_dim.10), calls=%async_computation.1 | async-start | bytes 1048576 | tf_op jit(solution)/shard_map/all_to_all | solution.py:514
  103.9 0.8 copy-start
  108.3 0.9 copy-start.9

commit v3 on v2

--- a/solution.py
+++ b/solution.py
@@ -279,7 +279,7 @@
                     total = act if total is None else total + act
             ci[i, 2 * j + half] = (pair_sum(total) * 0.125).astype(BF16)
 
-    pipelined((nx + 12) // 2 * pairs, 5, second_product, second_finish, even, odd)
+    pipelined((nx + 12) // 2 * pairs, 10, second_product, second_finish, even, odd)
 
     cx, cy = nx // 2, ny // 2
     coarse_pairs = (cy + 4) // 4
@@ -312,7 +312,7 @@
             for dy in range(2 * blocks):
                 pg[2 * i + dx, dy] = column_of(product, dx, dy, 2)
 
-    @pl.loop(0, nx + 2, unroll=3)
+    @pl.loop(0, nx + 2, unroll=6)
     def _(x):
         up = (x + 1) // 2
         for y in range(ny + 2):

time: 111 us -> 110 us (level)
  no operation moved by 1% of the time
where the time goes in v3:
time: 110 us; the launch traced here: 109 us
  Pallas kernels  37.7 us (34%)
  blocking collectives  26 us (24%)
  starting transfers between devices  16.8 us (15%)
  local copies, waits for them, and re-layouts  13.3 us (12%)
  waiting for transfers between devices  13 us (12%)
  other arithmetic  1.18 us (1%)
    pallas_call x1, Pallas kernels, body(): pl.pallas_call(lambda *refs: step_kernel(scale, nx, ny, *refs), out_shape...  28.8 us
    all_to_all x1, blocking collectives, body(): lax.all_to_all(grads.reshape(devices, -1, LANES), AXES, 0, 0, tiled=True)  26 us
    ppermute x6, starting transfers between devices, shifted(): lax.ppermute(block, axis, [(i, (i + steps) % count) for i in range(count)])  12.9 us
    all_to_all x1, waiting for transfers between devices, body(): total = lax.all_to_all(total, AXES, 0, 0, tiled=True).reshape(2048, LANES)  8.54 us
    unnamed x35, local copies, waits for them, and re-layouts  4.59 us
    ppermute x6, waiting for transfers between devices, shifted(): lax.ppermute(block, axis, [(i, (i + steps) % count) for i in range(count)])  4.44 us
    all_to_all x1, starting transfers between devices, body(): total = lax.all_to_all(total, AXES, 0, 0, tiled=True).reshape(2048, LANES)  3.97 us
    pallas_call x1, Pallas kernels, body(): pl.pallas_call(weights_kernel, out_shape=[jax.ShapeDtypeStruct((6 * CH, 1...  3.68 us
  transfers between devices with their start and end apart: 7, of which 4 were waited for; matrix products, arithmetic and copies ran while one was open for 7% of the time, Pallas kernels for 6%

profile of v3, /device:TPU:1, one launch (start us, length us, event | category | flops | bytes accessed | tf_op | source)
XLA Modules:
  0.0 108.9 jit_solution(895139072001804841)
XLA Ops:
  0.6 0.8 copy.26
  1.5 0.1 maximum_bitcast_fusion.1.own_ref
  1.6 4.2 %collective-permute-start = (bf16[4,8,8,128]{3,2,1,0:T(8,128)(2,1)S(1)}, bf16[4,8,8,128]{3,2,1,0:T(8,128)(2,1)S(1)}, u32[]{:S(2)}, u32[]{:S(2)}) collective-permute-start(bf16[4,8,8,128]{3,2,1,0:T(8,128)(2,1)S(1)} %maximum_bitcast_fusion.1.own_ref), channel_id=1, source_target_pairs={{0,1},{1,2},{2,3},{3,0},{4,5},{5,6},{6,7},{7,4},{8,9},{9,10},{10,1... | collective-permute-start | bytes 196616 | tf_op jit(solution)/shard_map/ppermute | solution.py:22
  5.8 0.0 copy-start.11
  5.9 0.7 copy-done.11
  6.6 0.1 pad_maximum_fusion.4
  6.7 0.1 pad_bitcast_fusion.5
  6.8 0.3 collective-permute-done
  7.1 3.9 %collective-permute-done.1 = bf16[4,8,8,128]{3,2,1,0:T(8,128)(2,1)S(1)} collective-permute-done((bf16[4,8,8,128]{3,2,1,0:T(8,128)(2,1)S(1)}, bf16[4,8,8,128]{3,2,1,0:T(8,128)(2,1)S(1)}, u32[]{:S(2)}, u32[]{:S(2)}) %collective-permute-start.1) | collective-permute-done | bytes 65568 | tf_op jit(solution)/shard_map/ppermute | solution.py:22
  11.0 3.0 %collective-permute-start.2 = (bf16[4,24,8,128]{3,2,1,0:T(8,128)(2,1)S(1)}, bf16[4,24,8,128]{3,2,1,0:T(8,128)(2,1)S(1)}, u32[]{:S(2)}, u32[]{:S(2)}) collective-permute-start(bf16[4,24,8,128]{3,2,1,0:T(8,128)(2,1)S(1)} %pad_maximum_fusion.2.refs_2_), channel_id=1, source_target_pairs={{0,8},{4,12},{8,16},{12,20},{16,24},{20,28},{24,32},{28,36},{32,40... | collective-permute-start | bytes 589832 | tf_op jit(solution)/shard_map/ppermute | solution.py:22
  14.0 0.4 collective-permute-start.3
  14.4 5.3 %collective-permute-start.4 = (bf16[4,24,8,128]{3,2,1,0:T(8,128)(2,1)S(1)}, bf16[4,24,8,128]{3,2,1,0:T(8,128)(2,1)S(1)}, u32[]{:S(2)}, u32[]{:S(2)}) collective-permute-start(bf16[4,24,8,128]{3,2,1,0:T(8,128)(2,1)S(1)} %pad_maximum_fusion.2.refs_2_), channel_id=1, source_target_pairs={{0,124},{4,0},{8,4},{12,8},{16,12},{20,16},{24,20},{28,24},{32,28}... | collective-permute-start | bytes 589832 | tf_op jit(solution)/shard_map/ppermute | solution.py:22
  19.7 0.1 pad_maximum_fusion.1
  19.8 0.2 copy.31
  20.0 0.2 reshape.45
  20.2 0.8 copy.33.refs_10_
  21.0 0.1 pad_maximum_fusion
  21.0 0.2 copy.29
  21.3 0.2 reshape.42
  21.5 0.8 copy.32.refs_5_
  22.3 1.2 %reshape.43.two_ref = bf16[27,64,64]{2,1,0:T(8,128)(2,1)} reshape(bf16[27,4096]{1,0:T(8,128)(2,1)S(1)} %copy-done.3) | data formatting | bytes 442368 | tf_op jit(solution)/shard_map/reshape | solution.py:444
  23.5 1.2 %reshape.44.three_ref = bf16[27,64,64]{2,1,0:T(8,128)(2,1)} reshape(bf16[27,4096]{1,0:T(8,128)(2,1)S(1)} %copy-done.4) | data formatting | bytes 442368 | tf_op jit(solution)/shard_map/reshape | solution.py:444
  24.7 3.7 %shard_map.101 = (bf16[384,768]{1,0:T(8,128)(2,1)}, bf16[384,768]{1,0:T(8,128)(2,1)}, bf16[384,768]{1,0:T(8,128)(2,1)}, bf16[384,768]{1,0:T(8,128)(2,1)}) custom-call(bf16[27,64,64]{2,1,0:T(8,128)(2,1)} %reshape.43.two_ref, bf16[27,64,64]{2,1,0:T(8,128)(2,1)} %reshape.44.three_ref), custom_call_target="tpu_custom_call" | custom-call | bytes 30000000 | tf_op jit(solution)/shard_map/pallas_call | solution.py:438
  28.4 0.2 collective-permute-done.5.refs_4_
  28.7 0.4 copy-done.5
  29.1 0.1 copy-done.6
  29.1 0.1 copy-done.7
  29.2 0.2 copy-done.8
  29.4 28.8 %shard_map.102 = (bf16[6,10,64,128]{3,2,1,0:T(8,128)(2,1)}, bf16[2048,128]{1,0:T(8,128)(2,1)}) custom-call(bf16[4,24,8,128]{3,2,1,0:T(8,128)(2,1)} %copy-done.5, bf16[4,24,8,128]{3,2,1,0:T(8,128)(2,1)} %copy-done.6, bf16[4,24,8,128]{3,2,1,0:T(8,128)(2,1)} %copy-done.1, bf16[4,24,8,128]{3,2,1,0:T(8,128)(2,1)} %copy-done.7, bf16[4,24,8,128]{3,2,1,0:T(8,128)(2,1)} %copy-done.8, ...), custom_call_target="tpu_custom_call" | custom-call | tf_op jit(solution)/shard_map/pallas_call | solution.py:464
  58.1 26.0 %all_to_all.10 = bf16[128,16,128]{2,1,0:T(8,128)(2,1)S(1)} all-to-all(bf16[128,16,128]{2,1,0:T(8,128)(2,1)} %bitcast.59), channel_id=1, replica_groups=mesh['gx'=32,'gy'=4] {'gx','gy'}, dimensions={0} | all-to-all | bytes 1048576 | tf_op jit(solution)/shard_map/all_to_all | solution.py:511
  84.1 0.1 reduce_sum.12
  84.3 0.9 broadcast_in_dim.10
  85.1 4.0 %all-to-all-start.1 = ((bf16[128,16,128]{2,1,0:T(8,128)(2,1)}), bf16[128,16,128]{2,1,0:T(8,128)(2,1)S(1)}, u32[]{:S(2)}, u32[]{:S(2)}) async-start(bf16[128,16,128]{2,1,0:T(8,128)(2,1)} %broadcast_in_dim.10), calls=%async_computation.1 | async-start | bytes 1048576 | tf_op jit(solution)/shard_map/all_to_all | solution.py:514
  89.2 0.1 copy.34
  89.3 0.8 reshape.46.t4_ref
  90.0 2.8 %shard_map.103 = f32[4,8,8,128]{3,2,1,0:T(8,128)} custom-call(bf16[6,10,64,128]{3,2,1,0:T(8,128)(2,1)} %get-tuple-element.25.sk, bf16[4,8,8,128]{3,2,1,0:T(8,128)(2,1)} %copy-done.2, bf16[48,768]{1,0:T(8,128)(2,1)} %reshape.46.t4_ref), custom_call_target="tpu_custom_call" | custom-call | flops 150994944 | bytes 2000000 | tf_op jit(solution)/shard_map/pallas_call | solution.py:500
  92.9 0.9 slice_bitcast_fusion
  93.8 0.6 copy.38
  94.4 8.5 %all-to-all-done.1 = bf16[128,16,128]{2,1,0:T(8,128)(2,1)S(1)} async-done(((bf16[128,16,128]{2,1,0:T(8,128)(2,1)}), bf16[128,16,128]{2,1,0:T(8,128)(2,1)S(1)}, u32[]{:S(2)}, u32[]{:S(2)}) %all-to-all-start.1) | async-done | bytes 524320 | tf_op jit(solution)/shard_map/all_to_all | solution.py:514
  102.9 0.8 copy-done
  103.8 2.4 %shard_map.104 = (f32[27,4096]{1,0:T(8,128)}, f32[27,4096]{1,0:T(8,128)}, f32[16,640]{1,0:T(8,128)}, f32[144,128]{1,0:T(8,128)}) custom-call(bf16[2048,128]{1,0:T(8,128)(2,1)} %bitcast.58), custom_call_target="tpu_custom_call" | custom-call | tf_op jit(solution)/shard_map/pallas_call | solution.py:516
  106.2 0.8 fusion.7
  107.0 0.1 stack.68
  107.1 0.1 stack.69
  107.2 0.1 stack.70
  107.3 0.6 copy.39
  107.9 0.2 copy-done.9
  108.3 0.7 maximum_bitcast_fusion.2
  (40 shorter events, 0.3 us)
Async XLA Ops:
  0.6 0.8 copy-start.12
  1.5 4.3 %copy-start.10 = (bf16[3,64,3,3,3]{1,4,3,2,0:T(4,128)(2,1)S(1)}, bf16[3,64,3,3,3]{1,4,3,2,0:T(4,128)(2,1)}, u32[]{:S(2)}) copy-start(bf16[3,64,3,3,3]{1,4,3,2,0:T(4,128)(2,1)} %param.11) | copy-start | bytes 31108
  1.6 9.4 %copy-start.2 = (bf16[4,8,8,128]{3,2,1,0:T(8,128)(2,1)}, bf16[4,8,8,128]{3,2,1,0:T(8,128)(2,1)S(1)}, u32[]{:S(2)}) copy-start(bf16[4,8,8,128]{3,2,1,0:T(8,128)(2,1)S(1)} %maximum_bitcast_fusion.1.own_ref) | copy-start | bytes 196612
  1.6 5.5 %collective-permute-start = (bf16[4,8,8,128]{3,2,1,0:T(8,128)(2,1)S(1)}, bf16[4,8,8,128]{3,2,1,0:T(8,128)(2,1)S(1)}, u32[]{:S(2)}, u32[]{:S(2)}) collective-permute-start(bf16[4,8,8,128]{3,2,1,0:T(8,128)(2,1)S(1)} %maximum_bitcast_fusion.1.own_ref), channel_id=1, source_target_pairs={{0,1},{1,2},{2,3},{3,0},{4,5},{5,6},{6,7},{7,4},{8,9},{9,10},{10,1... | collective-permute-start | bytes 196616 | tf_op jit(solution)/shard_map/ppermute | solution.py:22
  5.8 5.2 %collective-permute-start.1 = (bf16[4,8,8,128]{3,2,1,0:T(8,128)(2,1)S(1)}, bf16[4,8,8,128]{3,2,1,0:T(8,128)(2,1)S(1)}, u32[]{:S(2)}, u32[]{:S(2)}) collective-permute-start(bf16[4,8,8,128]{3,2,1,0:T(8,128)(2,1)S(1)} %maximum_bitcast_fusion.1.own_ref), channel_id=1, source_target_pairs={{0,3},{1,0},{2,1},{3,2},{4,7},{5,4},{6,5},{7,6},{8,11},{9,8},{10,9... | collective-permute-start | bytes 196616 | tf_op jit(solution)/shard_map/ppermute | solution.py:22
  5.8 0.7 copy-start.11
  11.0 8.8 %copy-start.1 = (bf16[4,24,8,128]{3,2,1,0:T(8,128)(2,1)}, bf16[4,24,8,128]{3,2,1,0:T(8,128)(2,1)S(1)}, u32[]{:S(2)}) copy-start(bf16[4,24,8,128]{3,2,1,0:T(8,128)(2,1)S(1)} %pad_maximum_fusion.2.refs_2_) | copy-start | bytes 589828
  11.0 17.4 %collective-permute-start.2 = (bf16[4,24,8,128]{3,2,1,0:T(8,128)(2,1)S(1)}, bf16[4,24,8,128]{3,2,1,0:T(8,128)(2,1)S(1)}, u32[]{:S(2)}, u32[]{:S(2)}) collective-permute-start(bf16[4,24,8,128]{3,2,1,0:T(8,128)(2,1)S(1)} %pad_maximum_fusion.2.refs_2_), channel_id=1, source_target_pairs={{0,8},{4,12},{8,16},{12,20},{16,24},{20,28},{24,32},{28,36},{32,40... | collective-permute-start | bytes 589832 | tf_op jit(solution)/shard_map/ppermute | solution.py:22
  14.0 14.4 %collective-permute-start.3 = (bf16[4,24,8,128]{3,2,1,0:T(8,128)(2,1)S(1)}, bf16[4,24,8,128]{3,2,1,0:T(8,128)(2,1)S(1)}, u32[]{:S(2)}, u32[]{:S(2)}) collective-permute-start(bf16[4,24,8,128]{3,2,1,0:T(8,128)(2,1)S(1)} %pad_maximum_fusion.2.refs_2_), channel_id=1, source_target_pairs={{0,4},{4,8},{8,12},{12,16},{16,20},{20,24},{24,28},{28,32},{32,36}... | collective-permute-start | bytes 589832 | tf_op jit(solution)/shard_map/ppermute | solution.py:22
  14.4 14.0 %collective-permute-start.4 = (bf16[4,24,8,128]{3,2,1,0:T(8,128)(2,1)S(1)}, bf16[4,24,8,128]{3,2,1,0:T(8,128)(2,1)S(1)}, u32[]{:S(2)}, u32[]{:S(2)}) collective-permute-start(bf16[4,24,8,128]{3,2,1,0:T(8,128)(2,1)S(1)} %pad_maximum_fusion.2.refs_2_), channel_id=1, source_target_pairs={{0,124},{4,0},{8,4},{12,8},{16,12},{20,16},{24,20},{28,24},{32,28}... | collective-permute-start | bytes 589832 | tf_op jit(solution)/shard_map/ppermute | solution.py:22
  19.7 9.0 %collective-permute-start.5 = (bf16[4,24,8,128]{3,2,1,0:T(8,128)(2,1)S(1)}, bf16[4,24,8,128]{3,2,1,0:T(8,128)(2,1)S(1)}, u32[]{:S(2)}, u32[]{:S(2)}) collective-permute-start(bf16[4,24,8,128]{3,2,1,0:T(8,128)(2,1)S(1)} %pad_maximum_fusion.2.refs_2_), channel_id=1, source_target_pairs={{0,120},{4,124},{8,0},{12,4},{16,8},{20,12},{24,16},{28,20},{32,24... | collective-permute-start | bytes 589832 | tf_op jit(solution)/shard_map/ppermute | solution.py:22
  21.3 1.0 copy-start.3
  22.2 1.2 %copy-start.4 = (bf16[27,4096]{1,0:T(8,128)(2,1)S(1)}, bf16[27,4096]{1,0:T(8,128)(2,1)}, u32[]{:S(2)}) copy-start(bf16[27,4096]{1,0:T(8,128)(2,1)} %param.10) | copy-start | bytes 663556
  28.4 0.7 copy-start.5
  28.4 0.7 copy-start.6
  28.4 0.8 copy-start.7
  28.7 0.7 copy-start.8
  85.1 17.8 %all-to-all-start.1 = ((bf16[128,16,128]{2,1,0:T(8,128)(2,1)}), bf16[128,16,128]{2,1,0:T(8,128)(2,1)S(1)}, u32[]{:S(2)}, u32[]{:S(2)}) async-start(bf16[128,16,128]{2,1,0:T(8,128)(2,1)} %broadcast_in_dim.10), calls=%async_computation.1 | async-start | bytes 1048576 | tf_op jit(solution)/shard_map/all_to_all | solution.py:514
  102.9 0.8 copy-start
  107.3 0.9 copy-start.9
